TPU v7x, 256 devices: a whole 4x4x8 slice. The times are simulated.
256 devices in a mesh: kvp: 64 (over z, x, core), section: 4 (over y).
Axes of the slice: x: 4, y: 4, z: 8, core: 2. Of those that a mesh axis runs over, the one named last changes fastest.
Arguments:
- hidden: bfloat16 [4, 128, 8192], P('section', 'kvp'), may hold values from -15 to 15
- norm_gain: bfloat16 [4, 8192], P('section'), may hold values from 0.099609375 to 1.8984375
- w_query: bfloat16 [4, 8192, 8192], P('section', None, 'kvp'), may hold values from -0.0625 to 0.0625
- w_kv: bfloat16 [4, 8192, 2048], P('section', None, 'kvp'), may hold values from -0.3125 to 0.3125
- w_out: bfloat16 [4, 8192, 8192], P('section', 'kvp'), may hold values from -0.0625 to 0.0625
- doc_cache: bfloat16 [4, 256, 128, 2048], P('section', 'kvp'), may hold values from -470 to 470
- page_table: int32 [4, 64, 4], P('section', 'kvp'), may hold values from 0 to 3, as said below
- page_count: int32 [4, 64], P('section', 'kvp'), may hold values from 1 to 4, as said below
Outputs:
- next_hidden: bfloat16 [4, 128, 8192], P('section', 'kvp')
Inputs may be any that keep to these rules, and one draw needn't show every extreme that they name: Each row page_table[s, k] is an ordering of all slots 0 to 3 of that device's pool. `page_count`: in every section one device has all 4 pages live; the others have 1 to 4, unevenly.
All inputs are finite; a program needn't handle non-finite values.
Results may differ from a plain program's by a relative error of at most 0.027.
The roundings to bfloat16 on the way count: a program that leaves them out, or rounds other values in their place, can miss the bound.
Values may be sent and summed in bfloat16 or wider, within the bound.
A program may use at most 128 MiB of HBM per device.

v0:
```python
import jax
import jax.numpy as jnp
from jax import lax
from jax.sharding import PartitionSpec as P

HEADS = 64
KVH = 8
HD = 128
PAGE = 128
PAGES_DEV = 4


epsilon = 1e-05
masked_score = -1e30


def shifted(value, axis, by):
    size = lax.axis_size(axis)
    return lax.ppermute(value, axis, [(i, (i + by) % size) for i in range(size)])


def normalize(incoming, gain_row):
    values = incoming.astype(jnp.float32)
    inv_rms = lax.rsqrt(jnp.mean(values * values, axis=-1, keepdims=True) + epsilon)
    return (values * inv_rms * gain_row.astype(jnp.float32)).astype(jnp.bfloat16)


def document_partial(grouped, pool, page_ids, live_count, blocks):
    block_pages = min(PAGES_DEV, max(1, 512 // PAGE))
    query_rows = grouped.shape[1]
    half_width = KVH * HD

    def block_step(block_index, state_now):
        run_max, run_sum, run_out = state_now
        first_slot = block_index * block_pages
        slot_live = first_slot + jnp.arange(block_pages, dtype=jnp.int32) < live_count
        page_rows = jnp.take(pool, page_ids, axis=0).reshape(block_pages * PAGE, 2 * half_width)
        doc_keys = page_rows[:, :half_width].reshape(block_pages * PAGE, KVH, HD)
        doc_values = page_rows[:, half_width:].reshape(block_pages * PAGE, KVH, HD)
        key_live = jnp.repeat(slot_live, PAGE)[None, None, :]
        scores = jnp.einsum(
            "kqd,nkd->kqn", grouped, doc_keys, preferred_element_type=jnp.float32
        ) * HD ** (-0.5)
        scores = jnp.where(key_live, scores, masked_score)
        block_max = jnp.max(scores, axis=-1)
        weights = jnp.where(key_live, jnp.exp(scores - block_max[..., None]), 0.0)
        block_sum = jnp.sum(weights, axis=-1)
        block_out = jnp.einsum(
            "kqn,nkd->kqd",
            weights.astype(jnp.bfloat16),
            doc_values,
            preferred_element_type=jnp.float32,
        )
        new_max = jnp.maximum(run_max, block_max)
        old_factor = jnp.exp(run_max - new_max)
        new_factor = jnp.exp(block_max - new_max)
        return (
            new_max,
            run_sum * old_factor + block_sum * new_factor,
            run_out * old_factor[..., None] + block_out * new_factor[..., None],
        )

    initial = (
        jnp.full((KVH, query_rows), masked_score, jnp.float32),
        jnp.zeros((KVH, query_rows), jnp.float32),
        jnp.zeros((KVH, query_rows, HD), jnp.float32),
    )
    return lax.fori_loop(0, blocks, block_step, initial)


def span_part(own_queries, own_keys, own_values):
    span_len = own_queries.shape[0]
    scores = jnp.einsum(
        "thd,uhd->htu", own_queries, own_keys, preferred_element_type=jnp.float32
    ) * HD ** (-0.5)
    causal = (jnp.arange(span_len)[:, None] >= jnp.arange(span_len)[None, :])[None]
    scores = jnp.where(causal, scores, masked_score)
    self_max = jnp.max(scores, axis=-1)
    weights = jnp.where(causal, jnp.exp(scores - self_max[..., None]), 0.0)
    self_sum = jnp.sum(weights, axis=-1)
    self_out = jnp.einsum(
        "htu,uhd->htd", weights.astype(jnp.bfloat16), own_values, preferred_element_type=jnp.float32
    )
    return (self_max, self_sum, self_out)


def local(hidden, norm_gain, w_query, w_kv, w_out, doc_cache, page_table, page_count):
    devices = lax.axis_size("kvp")
    position = lax.axis_index("kvp")
    group_size = HEADS // KVH
    own_heads = HEADS // devices
    resident = hidden[0]
    gathered = lax.all_gather(resident, "kvp", axis=0, tiled=True)
    span_len = gathered.shape[0]
    normed = normalize(gathered, norm_gain[0])
    query_part = jnp.dot(normed, w_query[0], preferred_element_type=jnp.float32).astype(
        jnp.bfloat16
    )
    fresh_part = jnp.dot(normed, w_kv[0], preferred_element_type=jnp.float32).astype(jnp.bfloat16)
    queries, fresh_rows = (
        lax.all_gather(query_part, "kvp", axis=1, tiled=True),
        lax.all_gather(fresh_part, "kvp", axis=1, tiled=True),
    )
    grouped = (
        queries.reshape(span_len, KVH, group_size, HD)
        .transpose(1, 2, 0, 3)
        .reshape(KVH, group_size * span_len, HD)
    )
    block_pages = min(PAGES_DEV, max(1, 512 // PAGE))
    live_count = page_count[0, 0]
    blocks = PAGES_DEV // block_pages
    part_max, part_sum, part_out = document_partial(
        grouped, doc_cache[0], page_table[0, 0], live_count, blocks
    )
    heads_max = part_max.reshape(HEADS, span_len)
    heads_sum = part_sum.reshape(HEADS, span_len)
    heads_out = part_out.reshape(HEADS, span_len, HD)
    first_head = position * own_heads
    global_max = lax.pmax(heads_max.astype(jnp.bfloat16), "kvp").astype(heads_max.dtype)
    factor = jnp.exp(heads_max - global_max)
    own_out, own_sum = (
        lax.psum_scatter(heads_out * factor[..., None], "kvp", scatter_dimension=0, tiled=True),
        lax.psum_scatter(heads_sum * factor, "kvp", scatter_dimension=0, tiled=True),
    )
    own_max = lax.dynamic_slice_in_dim(global_max, first_head, own_heads, 0)
    own_queries = lax.dynamic_slice_in_dim(
        queries.reshape(span_len, HEADS, HD), first_head, own_heads, 1
    )
    kv_heads = (first_head + jnp.arange(own_heads, dtype=jnp.int32)) // group_size
    new_keys = jnp.take(fresh_rows[:, : KVH * HD].reshape(span_len, KVH, HD), kv_heads, axis=1)
    new_values = jnp.take(fresh_rows[:, KVH * HD :].reshape(span_len, KVH, HD), kv_heads, axis=1)
    self_max, self_sum, self_out = span_part(own_queries, new_keys, new_values)
    top = jnp.maximum(own_max, self_max)
    doc_factor = jnp.exp(own_max - top)
    self_factor = jnp.exp(self_max - top)
    combined = (own_out * doc_factor[..., None] + self_out * self_factor[..., None]) / (
        own_sum * doc_factor + self_sum * self_factor
    )[..., None]
    attention = combined.transpose(1, 0, 2).reshape(span_len, own_heads * HD).astype(jnp.bfloat16)
    mixed = lax.psum_scatter(
        jnp.dot(attention, w_out[0], preferred_element_type=jnp.float32),
        "kvp",
        scatter_dimension=0,
        tiled=True,
    )
    updated = (resident.astype(jnp.float32) + mixed).astype(jnp.bfloat16)
    return shifted(updated[None], "section", 1)


def solution(mesh):
    placed = (
        P("section", "kvp", None),
        P("section", None),
        P("section", None, "kvp"),
        P("section", None, "kvp"),
        P("section", "kvp", None),
        P("section", "kvp", None, None),
        P("section", "kvp", None),
        P("section", "kvp"),
    )
    return jax.shard_map(
        local, mesh=mesh, in_specs=placed, out_specs=P("section", "kvp", None), check_vma=False
    )
```

profile of v0, /device:TPU:32, one launch (start us, length us, event | category | flops | bytes accessed | tf_op | source)
XLA Modules:
  0.0 968.3 jit_solution(13361245729114436360)
XLA Ops:
  6.5 1.6 copy.17
  9.0 81.9 %all-gather.6.cloned.1.call-done = bf16[1,128,8192]{2,0,1:T(2,128)(2,1)} async-done(((bf16[1,2,8192]{2,0,1:T(2,128)(2,1)}), bf16[1,128,8192]{2,0,1:T(2,128)(2,1)}) %all-gather.6.cloned.1.call-update) | async-done | bytes 2097168 | tf_op jit(solution)/shard_map/all_gather | solution.py:93
  90.9 6.5 convert_element_type.53
  97.4 3.0 fusion.6
  100.4 3.7 fusion.8
  104.2 1.3 copy-done.2
  105.5 1.5 fusion.20
  107.8 2.0 gather_fusion
  109.7 2.9 copy.27
  113.0 1.1 fusion.83
  114.1 63.4 %all-gather.4.cloned.1.call-done = bf16[128,8192]{1,0:T(8,128)(2,1)} async-done(((bf16[128,128]{1,0:T(8,128)(2,1)}), bf16[128,8192]{1,0:T(8,128)(2,1)}) %all-gather.4.cloned.1.call-update) | async-done | bytes 2097168 | tf_op jit(solution)/shard_map/all_gather | solution.py:101
  177.5 2.2 copy.30
  179.7 1.4 copy.18
  181.0 7.4 fusion
  188.5 233.1 %pmax.7 = bf16[64,128]{1,0:T(8,128)(2,1)S(1)} all-reduce(bf16[64,128]{1,0:T(8,128)(2,1)S(1)} %maximum_convert_fusion), channel_id=1, replica_groups=mesh['kvp'=64,'section'=4] {'kvp'}, use_global_device_ids=true, to_apply=%region_2.0 | all-reduce | flops 8192 | bytes 32768 | tf_op jit(solution)/shard_map/pmax | solution.py:119
  421.5 8.2 fusion.1
  429.8 9.7 %multiply_add_fusion = f32[8,1024,128]{2,1,0:T(8,128)S(1)} fusion(f32[8,1024]{1,0:T(8,128)S(1)} %get-tuple-element.54, f32[8,1024]{1,0:T(8,128)S(1)} %get-tuple-element.53, bf16[512,8,128]{0,2,1:T(8,128)(2,1)S(1)} %bitcast.117, f32[8,1024,512]{1,2,0:T(8,128)} %get-tuple-element.56, f32[8,1024]{1,0:T(8,128)S(1)} %get-tuple-element.55, ...), kind=kOutput, calls=%fused_computation.13 | convolution fusion | flops 1096810496 | bytes 22118912 | tf_op jit(solution)/shard_map/while/body/eval_jaxpr/kqn,nkd->kqd/dot_general | solution.py:48
  439.5 2.6 broadcast_multiply_fusion
  444.5 65.2 %all_gather.11 = bf16[128,2048]{0,1:T(8,128)(2,1)S(1)} all-gather(bf16[128,32]{0,1:T(8,128)(2,1)S(1)} %convolution_convert_fusion), channel_id=1, replica_groups=mesh['kvp'=64,'section'=4] {'kvp'}, dimensions={1}, use_global_device_ids=true | all-gather | bytes 532480 | tf_op jit(solution)/shard_map/all_gather | solution.py:102
  509.7 230.9 %all-reduce.1 = f32[64,128]{1,0:T(8,128)S(1)} all-reduce(f32[64,128]{1,0:T(8,128)S(1)} %get-tuple-element.51), channel_id=4, replica_groups=mesh['kvp'=64,'section'=4] {'kvp'}, use_global_device_ids=true, to_apply=%region_6.8.clone | all-reduce | flops 8192 | bytes 65536
  742.7 4.6 fusion.9
  748.0 207.0 %all-reduce.5.cloned.1.call-done = f32[128,8192]{1,0:T(8,128)} async-done(((f32[128,8192]{1,0:T(8,128)}), f32[128,8192]{1,0:T(8,128)}) %all-reduce.5.cloned.1.call-update) | async-done | bytes 4194320
  955.9 1.6 collective-permute-start
  957.5 3.6 collective-permute-done
  (54 shorter events, 7.5 us)
Async XLA Ops:
  6.5 101.2 %copy-start = (bf16[1,4,128,2048]{3,2,1,0:T(8,128)(2,1)S(1)}, bf16[1,4,128,2048]{3,2,1,0:T(8,128)(2,1)}, u32[]{:S(2)}) copy-start(bf16[1,4,128,2048]{3,2,1,0:T(8,128)(2,1)} %param.15) | copy-start | bytes 6291460
  6.5 84.4 %all-gather.6.cloned.1.call-start = ((), (), s32[]{:S(2)}) async-start(), calls=%async_computation.2 | async-start | bytes 4259840 | tf_op jit(solution)/shard_map/all_gather | solution.py:93
  8.1 169.3 %all-gather.4.cloned.1.call-start = ((), (), s32[]{:S(2)}) async-start(), calls=%async_computation.1 | async-start | bytes 2129920 | tf_op jit(solution)/shard_map/all_gather | solution.py:101
  100.4 5.1 copy-start.5
  100.4 7.3 copy-start.9
  104.1 1.3 copy-start.2
  107.0 635.6 %reduce-scatter.4.cloned.1.call-start = ((), (), s32[]{:S(2)}) async-start(), calls=%async_computation.4 | async-start | bytes 4259840
  179.6 8.8 copy-start.4
  421.5 8.2 copy-start.6
  442.1 0.7 copy-start.10
  442.1 1.6 copy-start.3
  442.1 1.7 copy-start.7
  442.1 512.8 %all-reduce.5.cloned.1.call-start = ((), (), s32[]{:S(2)}) async-start(), calls=%async_computation.3 | async-start | bytes 8388608
  742.7 219.1 %copy-start.1 = (bf16[1,4,128,2048]{3,2,1,0:T(8,128)(2,1)S(1)}, bf16[1,4,128,2048]{3,2,1,0:T(8,128)(2,1)}, u32[]{:S(2)}) copy-start(bf16[1,4,128,2048]{3,2,1,0:T(8,128)(2,1)} %param.15) | copy-start | bytes 6291460
  742.7 212.2 %copy-start.8 = (bf16[1,2,8192]{2,1,0:T(2,128)(2,1)S(1)}, bf16[1,2,8192]{2,1,0:T(2,128)(2,1)}, u32[]{:S(2)}) copy-start(bf16[1,2,8192]{2,1,0:T(2,128)(2,1)} %param.10) | copy-start | bytes 98308
  955.9 5.2 collective-permute-start
Sparse Core Ops, SparseCore 0:
  10.1 80.7 all-gather.5
  107.1 70.2 all-gather.3
  442.2 156.9 reduce-scatter.3
  747.4 207.4 all-reduce.4
where the time goes:
time: 971 us; the launch traced here: 968 us
  blocking collectives  529 us (54%)
  waiting for transfers between devices  356 us (37%)
  other arithmetic  26.7 us (3%)
  matrix products  24.3 us (3%)
  local copies, waits for them, and re-layouts  15.9 us (2%)
  between operations  14.7 us (2%)
    pmax x1, blocking collectives, local(): lax.pmax(heads_max.astype(jnp.bfloat16), 'kvp').astype(heads_max.dtype)  233 us
    unnamed x1, blocking collectives  231 us
    unnamed x6, waiting for transfers between devices  207 us
    all_gather x1, waiting for transfers between devices, local(): gathered = lax.all_gather(resident, 'kvp', axis=0, tiled=True)  81.9 us
    all_gather x1, blocking collectives, local(): lax.all_gather(fresh_part, 'kvp', axis=1, tiled=True)  65.2 us
    all_gather x1, waiting for transfers between devices, local(): lax.all_gather(query_part, 'kvp', axis=1, tiled=True)  63.4 us
  transfers between devices with their start and end apart: 5, of which 4 were waited for; matrix products, arithmetic and copies ran while one was open for 1% of the time, Pallas kernels for 0%

commit v1 on v0

v1 whole, which is shorter than its diff:
```python
import functools
import math

import jax
import jax.numpy as jnp
from jax import lax
from jax.experimental import pallas as pl
from jax.experimental.pallas import tpu as pltpu
from jax.sharding import PartitionSpec as P

MESH = pl.DeviceIdType.MESH
F32 = jnp.float32
BF16 = jnp.bfloat16

HD = 128
CORES = 2
RINGX = 4
SPLIT = 4
EXTRA = 16
EPSILON = 1e-05
BIG = 1e30
LOG2E = 1.4426950408889634


def dot(a, b, dims=((1,), (0,))):
    return lax.dot_general(a, b, (dims, ((), ())), preferred_element_type=F32)


def row_order(rows, nz, inverse):
    pieces = rows // (2 * nz)
    out_row = lax.broadcasted_iota(jnp.int32, (rows, rows), 0)
    in_row = lax.broadcasted_iota(jnp.int32, (rows, rows), 1)
    if inverse:
        out_row, in_row = in_row, out_row
    r = out_row % 2
    z = (out_row // 2) % nz
    piece = out_row // (2 * nz)
    return jnp.where(in_row == (z * pieces + piece) * 2 + r, 1.0, 0.0).astype(BF16)


def merge(parts):
    top = parts[0][1]
    for _, level in parts[1:]:
        top = jnp.maximum(top, level)
    total = None
    mixed = None
    for value, level in parts:
        weight = jnp.exp2(level - top)
        total = weight if total is None else total + weight
        mixed = value * weight if mixed is None else mixed + value * weight
    return mixed / total, top + jnp.log(total) * LOG2E


def packed(value, level):
    high = level.astype(BF16).astype(F32)
    middle = (level - high).astype(BF16).astype(F32)
    low = level - high - middle
    row = lax.broadcasted_iota(jnp.int32, (EXTRA, level.shape[1]), 0)
    tail = jnp.where(row == 0, high, jnp.where(row == 1, middle, jnp.where(row == 2, low, 0.0)))
    return value.astype(BF16), tail.astype(BF16)


def unpacked(message):
    return message[:HD].astype(F32), jnp.sum(message[HD:].astype(F32), axis=0, keepdims=True)


def kernel(
    n,
    nz,
    nx,
    sections,
    hid,
    gain,
    wq_hbm,
    wkv_hbm,
    wout_hbm,
    pool_hbm,
    table,
    count,
    out,
    wq,
    wkv,
    wout,
    kv,
    vt,
    stage_x,
    stage_n,
    stage_o,
    gbuf,
    xbuf,
    qbuf,
    fown,
    fbuf,
    ocs,
    ocr,
    own_out,
    own_level,
    oxs,
    oxr,
    ozs,
    ozr,
    att,
    ycs,
    ycr,
    yown,
    yxs,
    yxr,
    yzs,
    yzr,
    fin,
    finr,
    load_sem,
    kv_sem,
    az_s,
    az_r,
    ax_s,
    ax_r,
    ac_s,
    ac_r,
    qz_s,
    qz_r,
    qx_s,
    qx_r,
    qc_s,
    qc_r,
    f_s,
    f_r,
    oc_s,
    oc_r,
    ox_s,
    ox_r,
    oz_s,
    oz_r,
    yc_s,
    yc_r,
    yx_s,
    yx_r,
    yz_s,
    yz_r,
    sec_s,
    sec_r,
):
    kvh = nz
    span = 2 * n
    model = hid.shape[-1]
    wide = model // SPLIT
    thin = wide // 8
    pages = pool_hbm.shape[1]
    scale = HD ** (-0.5) * LOG2E

    me = lax.axis_index("kvp")
    section = lax.axis_index("section")
    c = me % CORES
    x = (me // CORES) % nx
    z = me // (CORES * nx)
    half = n // 2
    fresh_head = (me % half) // nx
    fresh_piece = (me // half) * nx + me % nx

    def at(zz, xx, cc):
        return (zz * nx + xx) * CORES + cc

    def remote(src, dst, send, recv, target):
        return pltpu.make_async_remote_copy(
            src_ref=src,
            dst_ref=dst,
            send_sem=send,
            recv_sem=recv,
            device_id={"kvp": target},
            device_id_type=MESH,
        )

    def to_z(d):
        return at((z + d) % nz, x, c)

    def to_x(d):
        return at(z, (x + d) % nx, c)

    peer = at(z, x, 1 - c)

    loads = [
        pltpu.make_async_copy(wq_hbm.at[0], wq, load_sem.at[0]),
        pltpu.make_async_copy(wkv_hbm.at[0], wkv, load_sem.at[1]),
        pltpu.make_async_copy(wout_hbm.at[0], wout, load_sem.at[2]),
    ]
    kv_loads = [
        pltpu.make_async_copy(pool_hbm.at[0, :, :, pl.ds(i * HD, HD)], kv.at[i], kv_sem.at[i])
        for i in range(2 * kvh)
    ]
    for load in loads[:2] + kv_loads + loads[2:]:
        load.start()

    barrier = pltpu.get_barrier_semaphore()

    def greet(target):
        pl.semaphore_signal(barrier, inc=1, device_id={"kvp": target}, device_id_type=MESH)

    for d in range(1, nz):
        greet(to_z(d))
    for d in range(1, nx):
        greet(to_x(d))
    greet(peer)
    for i in range(2 * nx):
        source = (i // nx) * half + z * nx + i % nx

        @pl.when(source != me)
        def _():
            greet(source)

    pl.semaphore_signal(
        barrier,
        inc=1,
        device_id={"section": (section + sections - 1) % sections},
        device_id_type=MESH,
    )

    values = hid[0].astype(F32)
    inv_rms = lax.rsqrt(jnp.mean(values * values, axis=-1, keepdims=True) + EPSILON)
    normed = (values * inv_rms * gain[...].astype(F32)).astype(BF16).astype(F32)
    for q in range(SPLIT):
        for j in range(8):
            start = q * wide + j * thin
            stage_n[q, 2 * j : 2 * j + 2, :] = normed[:, start : start + thin]
            stage_x[q, 2 * j : 2 * j + 2, :] = values[:, start : start + thin]
    for q in range(SPLIT):
        gbuf[q, z] = stage_n[q].astype(BF16)

    own_target = jnp.where(fresh_head == z, 1, 0)
    pl.semaphore_wait(barrier, (nz - 1) + (nx - 1) + 1 + 2 * nx + 1 - own_target)

    def az(q, d):
        return remote(gbuf.at[q, z], gbuf.at[q, z], az_s.at[q, d - 1], az_r.at[q, d - 1], to_z(d))

    def az_in(q, d):
        slot = gbuf.at[q, (z + nz - d) % nz]
        return remote(slot, slot, az_s.at[q, d - 1], az_r.at[q, d - 1], to_z(d))

    def ax(q, d):
        slot = xbuf.at[q, c, x]
        return remote(slot, slot, ax_s.at[q, d - 1], ax_r.at[q, d - 1], to_x(d))

    def ax_in(q, d):
        slot = xbuf.at[q, c, (x + nx - d) % nx]
        return remote(slot, slot, ax_s.at[q, d - 1], ax_r.at[q, d - 1], to_x(d))

    def ac(q):
        return remote(xbuf.at[q, c], xbuf.at[q, c], ac_s.at[q], ac_r.at[q], peer)

    def ac_in(q):
        return remote(xbuf.at[q, 1 - c], xbuf.at[q, 1 - c], ac_s.at[q], ac_r.at[q], peer)

    for q in range(SPLIT):
        for d in range(1, nz):
            az(q, d).start()

    for load in kv_loads:
        load.wait()

    @pl.loop(0, kvh)
    def _(g):
        vt[g] = kv[kvh + g].reshape(pages * HD, HD).T

    spread = row_order(16 * nz, nz, False)
    gather = row_order(16 * nz, nz, True)
    loads[0].wait()
    loads[1].wait()

    query = jnp.zeros((span, HD), F32)
    fresh = jnp.zeros((wkv.shape[0], span), F32)
    for t in range(SPLIT + 2):
        if t < SPLIT:
            for d in range(1, nz):
                az_in(t, d).wait_recv()
            rows = dot(spread, gbuf[t].reshape(16 * nz, thin)).astype(BF16)
            for j in range(8):
                xbuf[t, c, x, :, j * thin : (j + 1) * thin] = rows[j * 2 * nz : (j + 1) * 2 * nz]
            for d in range(1, nx):
                ax(t, d).start()
        if 1 <= t <= SPLIT:
            for d in range(1, nx):
                ax_in(t - 1, d).wait_recv()
            ac(t - 1).start()
        if t >= 2:
            q = t - 2
            ac_in(q).wait_recv()
            block = xbuf[q].reshape(span, wide)
            query = query + dot(block, wq[q * wide : (q + 1) * wide])
            fresh = fresh + dot(wkv[:, q * wide : (q + 1) * wide], block, ((1,), (1,)))

    qbuf[z, c, x] = query.T.astype(BF16)
    fown[...] = fresh.astype(BF16)

    def qz(d):
        slot = qbuf.at[z, c, x]
        return remote(slot, slot, qz_s.at[d - 1], qz_r.at[d - 1], to_z(d))

    def qz_in(g, d):
        slot = qbuf.at[g, c, x]
        return remote(slot, slot, qz_s.at[d - 1], qz_r.at[d - 1], to_z(d))

    def qx(g, d):
        slot = qbuf.at[g, c, x]
        return remote(slot, slot, qx_s.at[g, d - 1], qx_r.at[g, d - 1], to_x(d))

    def qx_in(g, d):
        slot = qbuf.at[g, c, (x + nx - d) % nx]
        return remote(slot, slot, qx_s.at[g, d - 1], qx_r.at[g, d - 1], to_x(d))

    def qc(g):
        return remote(qbuf.at[g, c], qbuf.at[g, c], qc_s.at[g], qc_r.at[g], peer)

    def qc_in(g):
        return remote(qbuf.at[g, 1 - c], qbuf.at[g, 1 - c], qc_s.at[g], qc_r.at[g], peer)

    def fresh_out(i):
        return remote(
            fown,
            fbuf.at[fresh_piece],
            f_s.at[i],
            f_r.at[fresh_piece],
            fresh_head * CORES * nx + i,
        )

    for d in range(1, nz):
        qz(d).start()
    for i in range(2 * nx):
        target = fresh_head * CORES * nx + i

        @pl.when(target != me)
        def _():
            fresh_out(i).start()

        @pl.when(target == me)
        def _():
            pltpu.make_async_copy(fown, fbuf.at[fresh_piece], f_r.at[fresh_piece]).start()

    bounds = []
    for slot in range(pages):
        bound = jnp.float32(BIG)
        for j in range(pages):
            named = jnp.logical_and(table[0, 0, j] == slot, j < count[0, 0])
            bound = jnp.where(named, jnp.float32(-BIG), bound)
        bounds.append(bound)

    def attend(g, side):
        cols = jnp.concatenate([qbuf[g, side, i] for i in range(nx)], axis=1)
        scores = dot(kv[g].reshape(pages * HD, HD), cols)
        parts = [scores[p * HD : (p + 1) * HD] for p in range(pages)]
        top = None
        for part, bound in zip(parts, bounds):
            here = jnp.minimum(jnp.max(part, axis=0, keepdims=True), -bound)
            top = here if top is None else jnp.maximum(top, here)
        total = None
        weights = []
        for part, bound in zip(parts, bounds):
            weight = jnp.exp2((part - jnp.maximum(top, bound)) * scale)
            add = jnp.sum(weight, axis=0, keepdims=True)
            total = add if total is None else total + add
            weights.append(weight.astype(BF16))
        mixed = dot(vt[g], jnp.concatenate(weights, axis=0))
        return mixed / total, top * scale + jnp.log(total) * LOG2E

    def oc(g):
        return remote(ocs.at[g], ocr.at[g], oc_s.at[g], oc_r.at[g], peer)

    def ox(g, d):
        return remote(
            oxs.at[g, (x + d) % nx], oxr.at[g, x], ox_s.at[g, d - 1], ox_r.at[g, d - 1], to_x(d)
        )

    def ox_in(g, d):
        slot = (x + nx - d) % nx
        return remote(
            oxs.at[g, slot], oxr.at[g, slot], ox_s.at[g, d - 1], ox_r.at[g, d - 1], to_x(d)
        )

    def oz(g, d):
        return remote(ozs.at[g], ozr.at[z], oz_s.at[d - 1], oz_r.at[d - 1], at(g, x, c))

    def oz_in(d):
        slot = (z + nz - d) % nz
        return remote(ozs.at[slot], ozr.at[slot], oz_s.at[d - 1], oz_r.at[d - 1], to_z(d))

    def offset(s):
        return (nz + ((s + 1) // 2) * (2 * (s % 2) - 1)) % nz

    @pl.loop(0, nz + 4)
    def _(t):
        @pl.when(t < nz)
        def _():
            d = offset(t)
            g = (z + d) % nz

            @pl.when(t > 0)
            def _():
                qz_in(g, nz - d).wait_recv()

            for e in range(1, nx):
                qx(g, e).start()

        @pl.when(jnp.logical_and(t >= 1, t < nz + 1))
        def _():
            g = (z + offset(t - 1)) % nz
            for e in range(1, nx):
                qx_in(g, e).wait_recv()
            qc(g).start()

        @pl.when(t >= 4)
        def _():
            d = offset(t - 4)
            g = (z + d) % nz
            for e in range(1, nx):
                ox_in(g, e).wait_recv()
            parts = [unpacked(oxs[g, x])]
            for e in range(1, nx):
                parts.append(unpacked(oxr[g, (x + e) % nx]))
            value, tail = packed(*merge(parts))
            ozs[g, :HD] = value
            ozs[g, HD:] = tail

            @pl.when(t > 4)
            def _():
                oz(g, d).start()

        @pl.when(jnp.logical_and(t >= 3, t < nz + 3))
        def _():
            g = (z + offset(t - 3)) % nz
            remote(ocs.at[g], ocr.at[g], oc_s.at[g], oc_r.at[g], peer).wait_recv()
            for i in range(nx):
                here = (own_out[:, i * span : (i + 1) * span], own_level[:, i * span : (i + 1) * span])
                value, tail = packed(*merge([here, unpacked(ocr[g, i])]))
                oxs[g, i, :HD] = value
                oxs[g, i, HD:] = tail
            for e in range(1, nx):
                ox(g, e).start()

        @pl.when(jnp.logical_and(t >= 2, t < nz + 2))
        def _():
            g = (z + offset(t - 2)) % nz
            qc_in(g).wait_recv()
            mixed, level = attend(g, 1 - c)
            for i in range(nx):
                value, tail = packed(
                    mixed[:, i * span : (i + 1) * span], level[:, i * span : (i + 1) * span]
                )
                ocs[g, i, :HD] = value
                ocs[g, i, HD:] = tail
            oc(g).start()
            mixed, level = attend(g, c)
            own_out[...] = mixed
            own_level[...] = level

    for i in range(2 * nx):
        remote(fown, fbuf.at[i], f_s.at[i], f_r.at[i], peer).wait_recv()
    new_keys = fbuf[:nx].reshape(HD, span)
    new_values = fbuf[nx:].reshape(HD, span)

    def token(axis):
        row = lax.broadcasted_iota(jnp.int32, (span, span), axis)
        r = row % 2
        tz = (row // 2) % nz
        tx = (row // (2 * nz)) % nx
        tc = row // (2 * nz * nx)
        return ((tz * nx + tx) * CORES + tc) * 2 + r

    causal = token(0) <= token(1)
    scores = dot(new_keys.T, qbuf[z, c, x])
    scores = jnp.where(causal, scores, -BIG)
    top = jnp.max(scores, axis=0, keepdims=True)
    weights = jnp.where(causal, jnp.exp2((scores - top) * scale), 0.0)
    total = jnp.sum(weights, axis=0, keepdims=True)
    own = dot(new_values, weights.astype(BF16)) / total
    parts = [(own, top * scale + jnp.log(total) * LOG2E), unpacked(ozs[z])]
    for d in range(1, nz):
        oz_in(d).wait_recv()
        parts.append(unpacked(ozr[(z + nz - d) % nz]))
    attention, _ = merge(parts)
    att[...] = attention.T.astype(BF16).reshape(CORES, span // CORES, HD)

    loads[2].wait()

    def yc(q):
        return remote(ycs.at[q], ycr.at[q], yc_s.at[q], yc_r.at[q], peer)

    def yx(q, d):
        return remote(
            yxs.at[q, (x + d) % nx], yxr.at[q, x], yx_s.at[q, d - 1], yx_r.at[q, d - 1], to_x(d)
        )

    def yx_in(q, d):
        slot = (x + nx - d) % nx
        return remote(
            yxs.at[q, slot], yxr.at[q, slot], yx_s.at[q, d - 1], yx_r.at[q, d - 1], to_x(d)
        )

    def yz(q, d):
        return remote(
            yzs.at[q, (z + d) % nz], yzr.at[q, z], yz_s.at[q, d - 1], yz_r.at[q, d - 1], to_z(d)
        )

    def yz_in(q, d):
        slot = (z + nz - d) % nz
        return remote(
            yzs.at[q, slot], yzr.at[q, slot], yz_s.at[q, d - 1], yz_r.at[q, d - 1], to_z(d)
        )

    def final(q):
        return pltpu.make_async_remote_copy(
            src_ref=fin.at[q],
            dst_ref=finr.at[q],
            send_sem=sec_s.at[q],
            recv_sem=sec_r.at[q],
            device_id={"section": (section + 1) % sections},
            device_id_type=MESH,
        )

    for t in range(SPLIT + 3):
        if t < SPLIT:
            weight = wout[:, t * wide : (t + 1) * wide]
            ycs[t] = dot(att[1 - c], weight).astype(BF16)
            yc(t).start()
            yown[t] = dot(att[c], weight)
        if 1 <= t <= SPLIT:
            q = t - 1
            yc(q).wait_recv()
            sums = yown[q] + ycr[q].astype(F32)
            yown[q] = sums
            yxs[q] = sums.astype(BF16).reshape(nx, 2 * nz, wide)
            for d in range(1, nx):
                yx(q, d).start()
        if 2 <= t <= SPLIT + 1:
            q = t - 2
            sums = yown[q, pl.ds(pl.multiple_of(x * 2 * nz, 2 * nz), 2 * nz)]
            for d in range(1, nx):
                yx_in(q, d).wait_recv()
                sums = sums + yxr[q, (x + nx - d) % nx].astype(F32)
            sums = sums.astype(BF16)
            rows = jnp.concatenate([sums[:, j * thin : (j + 1) * thin] for j in range(8)], axis=0)
            yzs[q] = dot(gather, rows).astype(BF16).reshape(nz, 16, thin)
            for d in range(1, nz):
                yz(q, d).start()
        if t >= 3:
            q = t - 3
            sums = yzs[q, z].astype(F32)
            for d in range(1, nz):
                yz_in(q, d).wait_recv()
                sums = sums + yzr[q, (z + nz - d) % nz].astype(F32)
            fin[q] = (stage_x[q] + sums).astype(BF16)
            final(q).start()

    for q in range(SPLIT):
        final(q).wait_recv()
        stage_o[...] = finr[q].astype(F32)
        for j in range(8):
            start = q * wide + j * thin
            out[0, :, start : start + thin] = stage_o[2 * j : 2 * j + 2, :].astype(BF16)

    for q in range(SPLIT):
        for d in range(1, nz):
            az(q, d).wait_send()
            yz(q, d).wait_send()
        for d in range(1, nx):
            ax(q, d).wait_send()
            yx(q, d).wait_send()
        ac(q).wait_send()
        yc(q).wait_send()
        final(q).wait_send()
    for d in range(1, nz):
        qz(d).wait_send()
        oz((z + d) % nz, d).wait_send()
    for g in range(nz):
        for d in range(1, nx):
            qx(g, d).wait_send()
            ox(g, d).wait_send()
        qc(g).wait_send()
        oc(g).wait_send()
    for i in range(2 * nx):

        @pl.when(fresh_head * CORES * nx + i != me)
        def _():
            fresh_out(i).wait_send()


def local(n, nx, sections, hidden, norm_gain, w_query, w_kv, w_out, doc_cache, page_table, page_count):
    nz = n // (CORES * nx)
    span = 2 * n
    model = hidden.shape[-1]
    wide = model // SPLIT
    thin = wide // 8
    fresh_rows = w_kv.shape[-1]
    pages = doc_cache.shape[1]
    tall = HD + EXTRA
    vmem = pl.BlockSpec(memory_space=pltpu.VMEM)
    smem = pl.BlockSpec(memory_space=pltpu.SMEM)
    anywhere = pl.BlockSpec(memory_space=pl.ANY)
    dma = pltpu.SemaphoreType.DMA

    def pair(*shape):
        return [dma(shape), dma(shape)]

    scratch = [
        pltpu.VMEM((model, HD), BF16),
        pltpu.VMEM((fresh_rows, model), BF16),
        pltpu.VMEM((HD, model), BF16),
        pltpu.VMEM((2 * nz, pages, HD, HD), BF16),
        pltpu.VMEM((nz, HD, pages * HD), BF16),
        pltpu.VMEM((SPLIT, 16, thin), F32),
        pltpu.VMEM((SPLIT, 16, thin), F32),
        pltpu.VMEM((16, thin), F32),
        pltpu.VMEM((SPLIT, nz, 16, thin), BF16),
        pltpu.VMEM((SPLIT, CORES, nx, 2 * nz, wide), BF16),
        pltpu.VMEM((nz, CORES, nx, HD, span), BF16),
        pltpu.VMEM((fresh_rows, span), BF16),
        pltpu.VMEM((2 * nx, fresh_rows, span), BF16),
        pltpu.VMEM((nz, nx, tall, span), BF16),
        pltpu.VMEM((nz, nx, tall, span), BF16),
        pltpu.VMEM((HD, nx * span), F32),
        pltpu.VMEM((1, nx * span), F32),
        pltpu.VMEM((nz, nx, tall, span), BF16),
        pltpu.VMEM((nz, nx, tall, span), BF16),
        pltpu.VMEM((nz, tall, span), BF16),
        pltpu.VMEM((nz, tall, span), BF16),
        pltpu.VMEM((CORES, span // CORES, HD), BF16),
        pltpu.VMEM((SPLIT, span // CORES, wide), BF16),
        pltpu.VMEM((SPLIT, span // CORES, wide), BF16),
        pltpu.VMEM((SPLIT, span // CORES, wide), F32),
        pltpu.VMEM((SPLIT, nx, 2 * nz, wide), BF16),
        pltpu.VMEM((SPLIT, nx, 2 * nz, wide), BF16),
        pltpu.VMEM((SPLIT, nz, 16, thin), BF16),
        pltpu.VMEM((SPLIT, nz, 16, thin), BF16),
        pltpu.VMEM((SPLIT, 16, thin), BF16),
        pltpu.VMEM((SPLIT, 16, thin), BF16),
        dma((3,)),
        dma((2 * nz,)),
        *pair(SPLIT, nz - 1),
        *pair(SPLIT, nx - 1),
        *pair(SPLIT),
        *pair(nz - 1),
        *pair(nz, nx - 1),
        *pair(nz),
        *pair(2 * nx),
        *pair(nz),
        *pair(nz, nx - 1),
        *pair(nz - 1),
        *pair(SPLIT),
        *pair(SPLIT, nx - 1),
        *pair(SPLIT, nz - 1),
        *pair(SPLIT),
    ]
    return pl.pallas_call(
        functools.partial(kernel, n, nz, nx, sections),
        out_shape=jax.ShapeDtypeStruct(hidden.shape, BF16),
        in_specs=[vmem, vmem, anywhere, anywhere, anywhere, anywhere, smem, smem],
        out_specs=vmem,
        scratch_shapes=scratch,
        compiler_params=pltpu.CompilerParams(
            collective_id=0, has_side_effects=True, vmem_limit_bytes=56 * 1024 * 1024
        ),
    )(hidden, norm_gain, w_query, jnp.swapaxes(w_kv, 1, 2), w_out, doc_cache, page_table, page_count)


def solution(mesh):
    placed = (
        P("section", "kvp", None),
        P("section", None),
        P("section", None, "kvp"),
        P("section", None, "kvp"),
        P("section", "kvp", None),
        P("section", "kvp", None, None),
        P("section", "kvp", None),
        P("section", "kvp"),
    )
    n = mesh.shape["kvp"]
    nx = RINGX if n >= 32 else 2
    return jax.shard_map(
        functools.partial(local, n, nx, mesh.shape["section"]),
        mesh=mesh,
        in_specs=placed,
        out_specs=P("section", "kvp", None),
        check_vma=False,
    )
```

time: 971 us -> 119 us (0.12)
  blocking collectives: 529 us -> 0 us
  waiting for transfers between devices: 356 us -> 0 us
  Pallas kernels: 0 us -> 116 us
  other arithmetic: 26.7 us -> 0 us
  matrix products: 24.3 us -> 0 us
  local copies, waits for them, and re-layouts: 15.9 us -> 1.4 us
  between operations: 14.7 us -> 0.66 us
    pmax x1 -> x0, blocking collectives: 233 us -> none  [local(): lax.pmax(heads_max.astype(jnp.bfloat16), 'kvp').astype(heads_max.dtype)]
    unnamed x1 -> x0, blocking collectives: 231 us -> none
    unnamed x6 -> x0, waiting for transfers between devices: 207 us -> none
    all_gather x2 -> x0, waiting for transfers between devices: 145 us -> none  [the longest x1 81.9 us: local(): gathered = lax.all_gather(resident, 'kvp', axis=0, tiled=True)]
    pallas_call x0 -> x1, Pallas kernels: none -> 116 us  [local(): pl.pallas_call(functools.partial(kernel, n, nz, nx, sections), out_shape=...]
    all_gather x1 -> x0, blocking collectives: 65.2 us -> none  [local(): lax.all_gather(fresh_part, 'kvp', axis=1, tiled=True)]
    dot_general x6 -> x0, matrix products: 24.3 us -> none  [the longest x1 9.71 us: block_step(): jnp.einsum('kqn,nkd->kqd', weights.astype(jnp.bfloat16), doc_values, pref...]
    reduce_sum x3 -> x0, other arithmetic: 11.2 us -> none  [the longest x1 8.16 us: block_step(): block_sum = jnp.sum(weights, axis=-1)]
  transfers between devices with their start and end apart: 5 -> 0, of which waited for: 4 -> 0; matrix products, arithmetic and copies ran while one was open for 1% -> 0% of each run, Pallas kernels for 0% -> 0%
where the time goes in v1:
time: 119 us; the launch traced here: 118 us
  Pallas kernels  116 us (97%)
  local copies, waits for them, and re-layouts  1.4 us (1%)
    pallas_call x1, Pallas kernels, local(): pl.pallas_call(functools.partial(kernel, n, nz, nx, sections), out_shape=...  116 us

profile of v1, /device:TPU:32, one launch (start us, length us, event | category | flops | bytes accessed | tf_op | source)
XLA Modules:
  0.0 118.4 jit_solution(9586636789356372973)
XLA Ops:
  0.7 116.3 %shard_map.82 = bf16[1,2,8192]{2,1,0:T(2,128)(2,1)} custom-call(bf16[1,2,8192]{2,1,0:T(2,128)(2,1)} %hid.1, bf16[1,8192]{1,0:T(2,128)(2,1)} %gain.1, bf16[1,8192,128]{2,1,0:T(8,128)(2,1)} %wq_hbm.1, bf16[1,32,8192]{2,1,0:T(8,128)(2,1)} %bitcast.1, bf16[1,128,8192]{2,1,0:T(8,128)(2,1)} %wout_hbm.1, bf16[1,4,128,2048]{3,2,1,0:T(8,128)(2,1)} %pool_hbm.1, ...), custom_call_target="tpu_custom_call" | custom-call | tf_op jit(solution)/shard_map/pallas_call | solution.py:650
  117.0 1.4 %copy.11 = bf16[1,2,8192]{2,1,0:T(2,128)(2,1)} copy(bf16[1,2,8192]{2,1,0:T(2,128)(2,1)} %shard_map.82) | data formatting | bytes 65536

commit v2 on v1

--- a/solution.py
+++ b/solution.py
@@ -20,6 +20,7 @@
 EPSILON = 1e-05
 BIG = 1e30
 LOG2E = 1.4426950408889634
+LAG = 5
 
 
 def dot(a, b, dims=((1,), (0,))):
@@ -207,12 +208,12 @@
         def _():
             greet(source)
 
-    pl.semaphore_signal(
-        barrier,
-        inc=1,
-        device_id={"section": (section + sections - 1) % sections},
-        device_id_type=MESH,
-    )
+    before = (section + sections - 1) % sections
+    after = (section + 1) % sections
+    for d in range(nz):
+        pl.semaphore_signal(
+            barrier, inc=1, device_id={"kvp": to_z(d), "section": before}, device_id_type=MESH
+        )
 
     values = hid[0].astype(F32)
     inv_rms = lax.rsqrt(jnp.mean(values * values, axis=-1, keepdims=True) + EPSILON)
@@ -224,9 +225,20 @@
             stage_x[q, 2 * j : 2 * j + 2, :] = values[:, start : start + thin]
     for q in range(SPLIT):
         gbuf[q, z] = stage_n[q].astype(BF16)
+        fin[q] = stage_x[q].astype(BF16)
 
     own_target = jnp.where(fresh_head == z, 1, 0)
-    pl.semaphore_wait(barrier, (nz - 1) + (nx - 1) + 1 + 2 * nx + 1 - own_target)
+    pl.semaphore_wait(barrier, (nz - 1) + (nx - 1) + 1 + 2 * nx + nz - own_target)
+
+    def residual():
+        return pltpu.make_async_remote_copy(
+            src_ref=fin,
+            dst_ref=finr,
+            send_sem=sec_s.at[0],
+            recv_sem=sec_r.at[0],
+            device_id={"section": after},
+            device_id_type=MESH,
+        )
 
     def az(q, d):
         return remote(gbuf.at[q, z], gbuf.at[q, z], az_s.at[q, d - 1], az_r.at[q, d - 1], to_z(d))
@@ -252,6 +264,8 @@
     for q in range(SPLIT):
         for d in range(1, nz):
             az(q, d).start()
+
+    residual().start()
 
     for load in kv_loads:
         load.wait()
@@ -384,48 +398,31 @@
     def offset(s):
         return (nz + ((s + 1) // 2) * (2 * (s % 2) - 1)) % nz
 
-    @pl.loop(0, nz + 4)
+    @pl.loop(0, nz)
+    def _(t):
+        d = offset(t)
+        g = (z + d) % nz
+
+        @pl.when(t > 0)
+        def _():
+            qz_in(g, nz - d).wait_recv()
+
+        for e in range(1, nx):
+            qx(g, e).start()
+
+    @pl.loop(0, nz + LAG)
     def _(t):
         @pl.when(t < nz)
         def _():
-            d = offset(t)
-            g = (z + d) % nz
-
-            @pl.when(t > 0)
-            def _():
-                qz_in(g, nz - d).wait_recv()
-
-            for e in range(1, nx):
-                qx(g, e).start()
-
-        @pl.when(jnp.logical_and(t >= 1, t < nz + 1))
-        def _():
-            g = (z + offset(t - 1)) % nz
+            g = (z + offset(t)) % nz
             for e in range(1, nx):
                 qx_in(g, e).wait_recv()
             qc(g).start()
 
-        @pl.when(t >= 4)
-        def _():
-            d = offset(t - 4)
-            g = (z + d) % nz
-            for e in range(1, nx):
-                ox_in(g, e).wait_recv()
-            parts = [unpacked(oxs[g, x])]
-            for e in range(1, nx):
-                parts.append(unpacked(oxr[g, (x + e) % nx]))
-            value, tail = packed(*merge(parts))
-            ozs[g, :HD] = value
-            ozs[g, HD:] = tail
-
-            @pl.when(t > 4)
-            def _():
-                oz(g, d).start()
-
-        @pl.when(jnp.logical_and(t >= 3, t < nz + 3))
-        def _():
-            g = (z + offset(t - 3)) % nz
-            remote(ocs.at[g], ocr.at[g], oc_s.at[g], oc_r.at[g], peer).wait_recv()
+        @pl.when(jnp.logical_and(t >= 2, t < nz + 2))
+        def _():
+            g = (z + offset(t - 2)) % nz
+            oc(g).wait_recv()
             for i in range(nx):
                 here = (own_out[:, i * span : (i + 1) * span], own_level[:, i * span : (i + 1) * span])
                 value, tail = packed(*merge([here, unpacked(ocr[g, i])]))
@@ -434,9 +431,9 @@
             for e in range(1, nx):
                 ox(g, e).start()
 
-        @pl.when(jnp.logical_and(t >= 2, t < nz + 2))
-        def _():
-            g = (z + offset(t - 2)) % nz
+        @pl.when(jnp.logical_and(t >= 1, t < nz + 1))
+        def _():
+            g = (z + offset(t - 1)) % nz
             qc_in(g).wait_recv()
             mixed, level = attend(g, 1 - c)
             for i in range(nx):
@@ -449,6 +446,23 @@
             mixed, level = attend(g, c)
             own_out[...] = mixed
             own_level[...] = level
+
+        @pl.when(t >= LAG)
+        def _():
+            d = offset(t - LAG)
+            g = (z + d) % nz
+            for e in range(1, nx):
+                ox_in(g, e).wait_recv()
+            parts = [unpacked(oxs[g, x])]
+            for e in range(1, nx):
+                parts.append(unpacked(oxr[g, (x + e) % nx]))
+            value, tail = packed(*merge(parts))
+            ozs[g, :HD] = value
+            ozs[g, HD:] = tail
+
+            @pl.when(t > LAG)
+            def _():
+                oz(g, d).start()
 
     for i in range(2 * nx):
         remote(fown, fbuf.at[i], f_s.at[i], f_r.at[i], peer).wait_recv()
@@ -494,27 +508,20 @@
         )
 
     def yz(q, d):
-        return remote(
-            yzs.at[q, (z + d) % nz], yzr.at[q, z], yz_s.at[q, d - 1], yz_r.at[q, d - 1], to_z(d)
+        return pltpu.make_async_remote_copy(
+            src_ref=yzs.at[q, (z + d) % nz],
+            dst_ref=yzr.at[q, z],
+            send_sem=yz_s.at[q, d],
+            recv_sem=yz_r.at[q, d],
+            device_id={"kvp": to_z(d), "section": after},
+            device_id_type=MESH,
         )
 
     def yz_in(q, d):
         slot = (z + nz - d) % nz
-        return remote(
-            yzs.at[q, slot], yzr.at[q, slot], yz_s.at[q, d - 1], yz_r.at[q, d - 1], to_z(d)
-        )
-
-    def final(q):
-        return pltpu.make_async_remote_copy(
-            src_ref=fin.at[q],
-            dst_ref=finr.at[q],
-            send_sem=sec_s.at[q],
-            recv_sem=sec_r.at[q],
-            device_id={"section": (section + 1) % sections},
-            device_id_type=MESH,
-        )
-
-    for t in range(SPLIT + 3):
+        return remote(yzs.at[q, slot], yzr.at[q, slot], yz_s.at[q, d], yz_r.at[q, d], peer)
+
+    for t in range(SPLIT + 2):
         if t < SPLIT:
             weight = wout[:, t * wide : (t + 1) * wide]
             ycs[t] = dot(att[1 - c], weight).astype(BF16)
@@ -537,20 +544,16 @@
             sums = sums.astype(BF16)
             rows = jnp.concatenate([sums[:, j * thin : (j + 1) * thin] for j in range(8)], axis=0)
             yzs[q] = dot(gather, rows).astype(BF16).reshape(nz, 16, thin)
-            for d in range(1, nz):
-                yz(q, d).start()
-        if t >= 3:
-            q = t - 3
-            sums = yzs[q, z].astype(F32)
-            for d in range(1, nz):
-                yz_in(q, d).wait_recv()
-                sums = sums + yzr[q, (z + nz - d) % nz].astype(F32)
-            fin[q] = (stage_x[q] + sums).astype(BF16)
-            final(q).start()
-
+            for d in range(nz):
+                yz(q, (d + 1) % nz).start()
+
+    residual().wait_recv()
     for q in range(SPLIT):
-        final(q).wait_recv()
-        stage_o[...] = finr[q].astype(F32)
+        sums = finr[q].astype(F32)
+        for d in range(nz):
+            yz_in(q, d).wait_recv()
+            sums = sums + yzr[q, (z + nz - d) % nz].astype(F32)
+        stage_o[...] = sums
         for j in range(8):
             start = q * wide + j * thin
             out[0, :, start : start + thin] = stage_o[2 * j : 2 * j + 2, :].astype(BF16)
@@ -558,13 +561,14 @@
     for q in range(SPLIT):
         for d in range(1, nz):
             az(q, d).wait_send()
+        for d in range(nz):
             yz(q, d).wait_send()
         for d in range(1, nx):
             ax(q, d).wait_send()
             yx(q, d).wait_send()
         ac(q).wait_send()
         yc(q).wait_send()
-        final(q).wait_send()
+    residual().wait_send()
     for d in range(1, nz):
         qz(d).wait_send()
         oz((z + d) % nz, d).wait_send()
@@ -644,8 +648,8 @@
         *pair(nz - 1),
         *pair(SPLIT),
         *pair(SPLIT, nx - 1),
-        *pair(SPLIT, nz - 1),
-        *pair(SPLIT),
+        *pair(SPLIT, nz),
+        *pair(1),
     ]
     return pl.pallas_call(
         functools.partial(kernel, n, nz, nx, sections),

time: 119 us -> 99.5 us (0.84)
  Pallas kernels: 116 us -> 96.4 us
    pallas_call x1, Pallas kernels: 116 us -> 96.4 us  [local(): pl.pallas_call(functools.partial(kernel, n, nz, nx, sections), out_shape=...]
where the time goes in v2:
time: 99.5 us; the launch traced here: 98.4 us
  Pallas kernels  96.4 us (97%)
  local copies, waits for them, and re-layouts  1.4 us (1%)
    pallas_call x1, Pallas kernels, local(): pl.pallas_call(functools.partial(kernel, n, nz, nx, sections), out_shape=...  96.4 us

profile of v2, /device:TPU:32, one launch (start us, length us, event | category | flops | bytes accessed | tf_op | source)
XLA Modules:
  0.0 98.4 jit_solution(6596248650876557944)
XLA Ops:
  0.7 96.4 %shard_map.82 = bf16[1,2,8192]{2,1,0:T(2,128)(2,1)} custom-call(bf16[1,2,8192]{2,1,0:T(2,128)(2,1)} %hid.1, bf16[1,8192]{1,0:T(2,128)(2,1)} %gain.1, bf16[1,8192,128]{2,1,0:T(8,128)(2,1)} %wq_hbm.1, bf16[1,32,8192]{2,1,0:T(8,128)(2,1)} %bitcast.1, bf16[1,128,8192]{2,1,0:T(8,128)(2,1)} %wout_hbm.1, bf16[1,4,128,2048]{3,2,1,0:T(8,128)(2,1)} %pool_hbm.1, ...), custom_call_target="tpu_custom_call" | custom-call | tf_op jit(solution)/shard_map/pallas_call | solution.py:654
  97.1 1.4 %copy.11 = bf16[1,2,8192]{2,1,0:T(2,128)(2,1)} copy(bf16[1,2,8192]{2,1,0:T(2,128)(2,1)} %shard_map.82) | data formatting | bytes 65536

commit v3 on v2

v3 whole, which is shorter than its diff:
```python
import functools
import math

import jax
import jax.numpy as jnp
from jax import lax
from jax.experimental import pallas as pl
from jax.experimental.pallas import tpu as pltpu
from jax.sharding import PartitionSpec as P

MESH = pl.DeviceIdType.MESH
F32 = jnp.float32
BF16 = jnp.bfloat16

HD = 128
CORES = 2
RINGX = 4
SPLIT = 4
MAIN = 96
EPSILON = 1e-05
BIG = 1e30
LOG2E = 1.4426950408889634
AHEAD = 3
PASS = 3
LAG = 8


def dot(a, b, dims=((1,), (0,))):
    return lax.dot_general(a, b, (dims, ((), ())), preferred_element_type=F32)


def row_order(rows, nz, inverse):
    pieces = rows // (2 * nz)
    out_row = lax.broadcasted_iota(jnp.int32, (rows, rows), 0)
    in_row = lax.broadcasted_iota(jnp.int32, (rows, rows), 1)
    if inverse:
        out_row, in_row = in_row, out_row
    r = out_row % 2
    z = (out_row // 2) % nz
    piece = out_row // (2 * nz)
    return jnp.where(in_row == (z * pieces + piece) * 2 + r, 1.0, 0.0).astype(BF16)


def merge(parts):
    top = parts[0][1]
    for _, level in parts[1:]:
        top = jnp.maximum(top, level)
    total = None
    mixed = None
    for value, level in parts:
        weight = jnp.exp2(level - top)
        total = weight if total is None else total + weight
        mixed = value * weight if mixed is None else mixed + value * weight
    return mixed * (1.0 / total), top + jnp.log(total) * LOG2E


def kernel(
    n,
    nz,
    nx,
    sections,
    hid,
    gain,
    wq_hbm,
    wkv_hbm,
    wout_hbm,
    pool_hbm,
    table,
    count,
    out,
    wq,
    wkv,
    wout,
    kv,
    vt,
    stage_x,
    stage_n,
    stage_o,
    gbuf,
    hbuf,
    xbuf,
    qbuf,
    fown,
    fbuf,
    ocs,
    ocr,
    lcs,
    lcr,
    own_out,
    own_level,
    oxs,
    oxr,
    lxs,
    lxr,
    ozs,
    ozr,
    lzs,
    lzr,
    pzs,
    pzr,
    mzs,
    mzr,
    pxs,
    pxr,
    mxs,
    mxr,
    att,
    ycs,
    ycr,
    yown,
    yxs,
    yxr,
    yzs,
    yzr,
    vzs,
    vzr,
    vxs,
    vxr,
    fin,
    finr,
    load_sem,
    kv_sem,
    az_s,
    az_r,
    ax_s,
    ax_r,
    ac_s,
    ac_r,
    hx_s,
    hx_r,
    hz_s,
    hz_r,
    qz_s,
    qz_r,
    qx_s,
    qx_r,
    qc_s,
    qc_r,
    rx_s,
    rx_r,
    rz_s,
    rz_r,
    f_s,
    f_r,
    oc_s,
    oc_r,
    lc_s,
    lc_r,
    ox_s,
    ox_r,
    lx_s,
    lx_r,
    oz_s,
    oz_r,
    lz_s,
    lz_r,
    pz_s,
    pz_r,
    mz_s,
    mz_r,
    px_s,
    px_r,
    mx_s,
    mx_r,
    yc_s,
    yc_r,
    yx_s,
    yx_r,
    yz_s,
    yz_r,
    vz_s,
    vz_r,
    vx_s,
    vx_r,
    sec_s,
    sec_r,
):
    kvh = nz
    span = 2 * n
    model = hid.shape[-1]
    wide = model // SPLIT
    thin = wide // 8
    pages = pool_hbm.shape[1]
    scale = HD ** (-0.5) * LOG2E

    me = lax.axis_index("kvp")
    section = lax.axis_index("section")
    c = me % CORES
    x = (me // CORES) % nx
    z = me // (CORES * nx)
    half = n // 2
    fresh_head = (me % half) // nx
    fresh_piece = (me // half) * nx + me % nx

    def at(zz, xx, cc):
        return (zz * nx + xx) * CORES + cc

    peer = at(z, x, 1 - c)

    def remote(src, dst, send, recv, target):
        return pltpu.make_async_remote_copy(
            src_ref=src,
            dst_ref=dst,
            send_sem=send,
            recv_sem=recv,
            device_id={"kvp": target},
            device_id_type=MESH,
        )

    def arrived(region, sem):
        remote(region, region, sem, sem, peer).wait_recv()

    def left(region, sem):
        remote(region, region, sem, sem, peer).wait_send()

    def to_z(d):
        return at((z + d) % nz, x, c)

    def to_x(d):
        return at(z, (x + d) % nx, c)

    loads = [
        pltpu.make_async_copy(wq_hbm.at[0], wq, load_sem.at[0]),
        pltpu.make_async_copy(wkv_hbm.at[0], wkv, load_sem.at[1]),
        pltpu.make_async_copy(wout_hbm.at[0], wout, load_sem.at[2]),
    ]
    kv_loads = [
        pltpu.make_async_copy(pool_hbm.at[0, :, :, pl.ds(i * HD, HD)], kv.at[i], kv_sem.at[0])
        for i in range(2 * kvh)
    ]
    for load in loads[:2] + kv_loads + loads[2:]:
        load.start()

    barrier = pltpu.get_barrier_semaphore()

    def greet(target):
        pl.semaphore_signal(barrier, inc=1, device_id={"kvp": target}, device_id_type=MESH)

    for d in range(1, nz):
        greet(to_z(d))
    for d in range(1, nx):
        greet(to_x(d))
    greet(peer)
    before = (section + sections - 1) % sections
    after = (section + 1) % sections
    pl.semaphore_signal(barrier, inc=1, device_id={"section": before}, device_id_type=MESH)

    values = hid[0].astype(F32)
    inv_rms = lax.rsqrt(jnp.mean(values * values, axis=-1, keepdims=True) + EPSILON)
    normed = (values * inv_rms * gain[...].astype(F32)).astype(BF16).astype(F32)
    for q in range(SPLIT):
        for j in range(8):
            start = q * wide + j * thin
            stage_n[q, 2 * j : 2 * j + 2, :] = normed[:, start : start + thin]
            stage_x[q, 2 * j : 2 * j + 2, :] = values[:, start : start + thin]
    for q in range(SPLIT):
        if q > 0:
            gbuf[q, z] = stage_n[q].astype(BF16)
        else:
            hbuf[z, x] = stage_n[q].astype(BF16)
        fin[q] = stage_x[q].astype(BF16)

    pl.semaphore_wait(barrier, (nz - 1) + (nx - 1) + 1 + 1)

    def residual():
        return pltpu.make_async_remote_copy(
            src_ref=fin,
            dst_ref=finr,
            send_sem=sec_s.at[0],
            recv_sem=sec_r.at[0],
            device_id={"section": after},
            device_id_type=MESH,
        )

    def az(q, d):
        return remote(gbuf.at[q, z], gbuf.at[q, z], az_s.at[0], az_r.at[q], to_z(d))

    def ax(q, d):
        slot = xbuf.at[q, c, x]
        return remote(slot, slot, ax_s.at[0], ax_r.at[q], to_x(d))

    def ac(q):
        return remote(xbuf.at[q, c], xbuf.at[q, c], ac_s.at[0], ac_r.at[q], peer)

    def hx(d):
        return remote(hbuf.at[z, x], hbuf.at[z, x], hx_s.at[0], hx_r.at[0], to_x(d))

    def hz(d):
        return remote(hbuf.at[z], hbuf.at[z], hz_s.at[0], hz_r.at[0], to_z(d))

    for d in range(1, nx):
        hx(d).start()
    for q in range(1, SPLIT):
        for d in range(1, nz):
            az(q, d).start()
    arrived(hbuf.at[0, pl.ds(0, nx - 1)], hx_r.at[0])
    for d in range(1, nz):
        hz(d).start()
    residual().start()

    pltpu.make_async_copy(kv, kv, kv_sem.at[0]).wait()

    @pl.loop(0, kvh)
    def _(g):
        vt[g] = kv[kvh + g].reshape(pages * HD, HD).T

    spread = row_order(16 * nz, nz, False)
    gather = row_order(16 * nz, nz, True)
    loads[0].wait()
    loads[1].wait()

    query = jnp.zeros((span, HD), F32)
    fresh = jnp.zeros((wkv.shape[0], span), F32)
    order = [*range(1, SPLIT), 0]
    for t in range(SPLIT + 2):
        if t < SPLIT - 1:
            q = order[t]
            arrived(gbuf.at[q, pl.ds(0, nz - 1)], az_r.at[q])
            rows = dot(spread, gbuf[q].reshape(16 * nz, thin)).astype(BF16)
            for j in range(8):
                xbuf[q, c, x, :, j * thin : (j + 1) * thin] = rows[j * 2 * nz : (j + 1) * 2 * nz]
            for d in range(1, nx):
                ax(q, d).start()
        elif t == SPLIT - 1:
            arrived(hbuf.at[pl.ds(0, nz - 1)], hz_r.at[0])
            for i in range(nx):
                block = jnp.concatenate([hbuf[k, i] for k in range(nz)], axis=0)
                rows = dot(spread, block).astype(BF16)
                for j in range(8):
                    xbuf[0, c, i, :, j * thin : (j + 1) * thin] = rows[j * 2 * nz : (j + 1) * 2 * nz]
            ac(0).start()
        if 1 <= t <= SPLIT - 1:
            q = order[t - 1]
            arrived(xbuf.at[q, 0, pl.ds(0, nx - 1)], ax_r.at[q])
            ac(q).start()
        if t >= 2:
            q = order[t - 2]
            arrived(xbuf.at[q, 0], ac_r.at[q])
            block = xbuf[q].reshape(span, wide)
            query = query + dot(block, wq[q * wide : (q + 1) * wide])
            fresh = fresh + dot(wkv[:, q * wide : (q + 1) * wide], block, ((1,), (1,)))

    qbuf[z, c, x] = query.T.astype(BF16)
    fown[...] = fresh.astype(BF16)

    def qz(d):
        slot = qbuf.at[z, c, x, pl.ds(0, MAIN)]
        return remote(slot, slot, qz_s.at[0], qz_r.at[d - 1], to_z(d))

    def qx(g, d):
        slot = qbuf.at[g, c, x, pl.ds(0, MAIN)]
        return remote(slot, slot, qx_s.at[0], qx_r.at[g], to_x(d))

    def rx(d):
        slot = qbuf.at[z, c, x, pl.ds(MAIN, HD - MAIN)]
        return remote(slot, slot, rx_s.at[0], rx_r.at[0], to_x(d))

    def rz(d):
        slot = qbuf.at[z, c, :, pl.ds(MAIN, HD - MAIN)]
        return remote(slot, slot, rz_s.at[0], rz_r.at[d - 1], to_z(d))

    def qc(g):
        return remote(qbuf.at[g, c], qbuf.at[g, c], qc_s.at[0], qc_r.at[g], peer)

    def fresh_out(i):
        return remote(
            fown,
            fbuf.at[fresh_piece],
            f_s.at[0],
            f_r.at[0],
            fresh_head * CORES * nx + i,
        )

    for d in range(1, nx):
        rx(d).start()
    for d in range(1, nz):
        qz(d).start()
    for d in range(1, nx):
        qx(z, d).start()
    for i in range(2 * nx):
        target = fresh_head * CORES * nx + i

        @pl.when(target != me)
        def _():
            fresh_out(i).start()

        @pl.when(target == me)
        def _():
            pltpu.make_async_copy(fown, fbuf.at[fresh_piece], f_r.at[0]).start()

    bounds = []
    for slot in range(pages):
        bound = jnp.float32(BIG)
        for j in range(pages):
            named = jnp.logical_and(table[0, 0, j] == slot, j < count[0, 0])
            bound = jnp.where(named, jnp.float32(-BIG), bound)
        bounds.append(bound)

    def attend(g, side):
        cols = jnp.concatenate([qbuf[g, side, i] for i in range(nx)], axis=1)
        scores = dot(kv[g].reshape(pages * HD, HD), cols)
        parts = [scores[p * HD : (p + 1) * HD] for p in range(pages)]
        top = None
        for part, bound in zip(parts, bounds):
            here = jnp.minimum(jnp.max(part, axis=0, keepdims=True), -bound)
            top = here if top is None else jnp.maximum(top, here)
        total = None
        weights = []
        for part, bound in zip(parts, bounds):
            weight = jnp.exp2((part - jnp.maximum(top, bound)) * scale)
            add = jnp.sum(weight, axis=0, keepdims=True)
            total = add if total is None else total + add
            weights.append(weight.astype(BF16))
        mixed = dot(vt[g], jnp.concatenate(weights, axis=0)) * (1.0 / total)
        return mixed, top * scale + jnp.log(total) * LOG2E

    def oc(g):
        return remote(ocs.at[g], ocr.at[g], oc_s.at[0], oc_r.at[g], peer)

    def lc(g):
        return remote(lcs.at[g], lcr.at[g], lc_s.at[0], lc_r.at[g], peer)

    def along_x(send, recv, send_sem, recv_sem):
        def out_copy(g, d):
            return remote(
                send.at[g, (x + d) % nx], recv.at[g, x], send_sem.at[0], recv_sem.at[g], to_x(d)
            )

        return out_copy, lambda g: arrived(recv.at[g, pl.ds(0, nx - 1)], recv_sem.at[g])

    def along_z(send, recv, send_sem, recv_sem):
        def out_copy(g):
            return remote(send.at[g], recv.at[z], send_sem.at[0], recv_sem.at[0], at(g, x, c))

        return out_copy, lambda: arrived(recv.at[pl.ds(0, nz - 1)], recv_sem.at[0])

    ox, ox_in = along_x(oxs, oxr, ox_s, ox_r)
    lx, lx_in = along_x(lxs, lxr, lx_s, lx_r)
    oz, oz_in = along_z(ozs, ozr, oz_s, oz_r)
    lz, lz_in = along_z(lzs, lzr, lz_s, lz_r)
    pz, pz_in = along_z(pzs, pzr, pz_s, pz_r)
    mz, mz_in = along_z(mzs, mzr, mz_s, mz_r)
    px, px_in = along_x(pxs, pxr, px_s, px_r)
    mx, mx_in = along_x(mxs, mxr, mx_s, mx_r)

    def offset(s):
        return (nz + ((s + 1) // 2) * (2 * (s % 2) - 1)) % nz

    def forward(s):
        d = offset(s)
        g = (z + d) % nz
        arrived(qbuf.at[g, 0, 0, pl.ds(0, MAIN)], qz_r.at[nz - d - 1])
        for e in range(1, nx):
            qx(g, e).start()

    arrived(qbuf.at[0, 0, pl.ds(0, nx - 1), pl.ds(MAIN, HD - MAIN)], rx_r.at[0])
    for d in range(1, nz):
        rz(d).start()
    for s in range(1, min(AHEAD, nz)):
        forward(s)

    @pl.loop(0, nz + LAG)
    def _(t):
        @pl.when(t < nz)
        def _():
            d = offset(t)
            g = (z + d) % nz
            arrived(qbuf.at[g, 0, pl.ds(0, nx - 1), pl.ds(0, MAIN)], qx_r.at[g])

            @pl.when(t > 0)
            def _():
                arrived(qbuf.at[g, 0, :, pl.ds(MAIN, HD - MAIN)], rz_r.at[nz - d - 1])

            qc(g).start()

        @pl.when(t < nz - AHEAD)
        def _():
            forward(t + AHEAD)

        @pl.when(jnp.logical_and(t >= PASS, t < nz + PASS))
        def _():
            d = offset(t - PASS)
            g = (z + d) % nz
            slot = (t - PASS) % (PASS - 1)
            arrived(ocr.at[g], oc_r.at[g])
            arrived(lcr.at[g], lc_r.at[g])
            for i in range(nx):
                cols = slice(i * span, (i + 1) * span)
                here = (own_out[slot, :, cols], own_level[slot, :, cols])
                value, level = merge([here, (ocr[g, i].astype(F32), lcr[g, i])])
                oxs[g, i] = value[:MAIN].astype(BF16)
                lxs[g, i] = level
                pzs[g, i] = value[MAIN:].astype(BF16)
                mzs[g, i] = level
            for e in range(1, nx):
                ox(g, e).start()
                lx(g, e).start()

            @pl.when(t > PASS)
            def _():
                pz(g).start()
                mz(g).start()

        @pl.when(jnp.logical_and(t >= 1, t < nz + 1))
        def _():
            g = (z + offset(t - 1)) % nz
            slot = (t - 1) % (PASS - 1)
            arrived(qbuf.at[g, 0], qc_r.at[g])
            mixed, level = attend(g, 1 - c)
            for i in range(nx):
                cols = slice(i * span, (i + 1) * span)
                ocs[g, i] = mixed[:, cols].astype(BF16)
                lcs[g, i] = level[:, cols]
            oc(g).start()
            lc(g).start()
            mixed, level = attend(g, c)
            own_out[slot] = mixed
            own_level[slot] = level

        @pl.when(t >= LAG)
        def _():
            d = offset(t - LAG)
            g = (z + d) % nz
            ox_in(g)
            lx_in(g)
            parts = [(oxs[g, x].astype(F32), lxs[g, x])]
            for e in range(1, nx):
                slot = (x + e) % nx
                parts.append((oxr[g, slot].astype(F32), lxr[g, slot]))
            value, level = merge(parts)
            ozs[g] = value.astype(BF16)
            lzs[g] = level

            @pl.when(t > LAG)
            def _():
                oz(g).start()
                lz(g).start()

    pz_in()
    mz_in()
    for i in range(nx):
        parts = [(pzs[z, i].astype(F32), mzs[z, i])]
        for d in range(1, nz):
            slot = (z + nz - d) % nz
            parts.append((pzr[slot, i].astype(F32), mzr[slot, i]))
        value, level = merge(parts)
        pxs[0, i] = value.astype(BF16)
        mxs[0, i] = level
    for e in range(1, nx):
        px(0, e).start()
        mx(0, e).start()

    arrived(fbuf, f_r.at[0])
    new_keys = fbuf[:nx].reshape(HD, span)
    new_values = fbuf[nx:].reshape(HD, span)

    def token(axis):
        row = lax.broadcasted_iota(jnp.int32, (span, span), axis)
        r = row % 2
        tz = (row // 2) % nz
        tx = (row // (2 * nz)) % nx
        tc = row // (2 * nz * nx)
        return ((tz * nx + tx) * CORES + tc) * 2 + r

    causal = token(0) <= token(1)
    scores = dot(new_keys.T, qbuf[z, c, x])
    scores = jnp.where(causal, scores, -BIG)
    top = jnp.max(scores, axis=0, keepdims=True)
    weights = jnp.where(causal, jnp.exp2((scores - top) * scale), 0.0)
    total = jnp.sum(weights, axis=0, keepdims=True)
    own = dot(new_values, weights.astype(BF16)) * (1.0 / total)
    own_lsum = top * scale + jnp.log(total) * LOG2E
    parts = [(own[:MAIN], own_lsum), (ozs[z].astype(F32), lzs[z])]
    oz_in()
    lz_in()
    for d in range(1, nz):
        slot = (z + nz - d) % nz
        parts.append((ozr[slot].astype(F32), lzr[slot]))
    first_rows, _ = merge(parts)
    parts = [(own[MAIN:], own_lsum), (pxs[0, x].astype(F32), mxs[0, x])]
    px_in(0)
    mx_in(0)
    for e in range(1, nx):
        slot = (x + nx - e) % nx
        parts.append((pxr[0, slot].astype(F32), mxr[0, slot]))
    last_rows, _ = merge(parts)
    attention = jnp.concatenate([first_rows, last_rows], axis=0)
    att[...] = attention.T.astype(BF16).reshape(CORES, span // CORES, HD)

    loads[2].wait()

    def yc(q):
        return remote(ycs.at[q], ycr.at[q], yc_s.at[0], yc_r.at[q], peer)

    def yx(q, d):
        return remote(
            yxs.at[q, (x + d) % nx], yxr.at[q, x], yx_s.at[0], yx_r.at[q], to_x(d)
        )

    def yz(q, d):
        return pltpu.make_async_remote_copy(
            src_ref=yzs.at[q, (z + d) % nz],
            dst_ref=yzr.at[q, z],
            send_sem=yz_s.at[0],
            recv_sem=yz_r.at[q],
            device_id={"kvp": to_z(d), "section": after},
            device_id_type=MESH,
        )

    def vz(d):
        return remote(vzs.at[(z + d) % nz], vzr.at[z], vz_s.at[0], vz_r.at[0], to_z(d))

    def vx(d):
        return pltpu.make_async_remote_copy(
            src_ref=vxs.at[(x + d) % nx],
            dst_ref=vxr.at[x],
            send_sem=vx_s.at[0],
            recv_sem=vx_r.at[0],
            device_id={"kvp": to_x(d), "section": after},
            device_id_type=MESH,
        )

    def by_owner(sums):
        rows = jnp.concatenate([sums[:, j * thin : (j + 1) * thin] for j in range(8)], axis=0)
        return dot(gather, rows).astype(BF16).reshape(nz, 16, thin)

    def sum_x(q):
        sums = yown[q, pl.ds(pl.multiple_of(x * 2 * nz, 2 * nz), 2 * nz)]
        arrived(yxr.at[q, pl.ds(0, nx - 1)], yx_r.at[q])
        for d in range(1, nx):
            sums = sums + yxr[q, (x + nx - d) % nx].astype(F32)
        yzs[q] = by_owner(sums.astype(BF16))
        for d in range(nz):
            yz(q, (d + 1) % nz).start()

    for t in range(SPLIT + 1):
        if t < SPLIT:
            weight = wout[:, t * wide : (t + 1) * wide]
            ycs[t] = dot(att[1 - c], weight).astype(BF16)
            yc(t).start()
            yown[t] = dot(att[c], weight)
        if t >= 1:
            q = t - 1
            arrived(ycr.at[q], yc_r.at[q])
            sums = yown[q] + ycr[q].astype(F32)
            blocks = sums.astype(BF16).reshape(nx, 2 * nz, wide)
            if q > 0:
                yown[q] = sums
                yxs[q] = blocks
                for d in range(1, nx):
                    yx(q, d).start()
            else:
                for i in range(nx):
                    vzs[:, i] = by_owner(blocks[i])
                for d in range(1, nz):
                    vz(d).start()
        if t >= 3:
            sum_x(t - 2)
    arrived(vzr.at[pl.ds(0, nz - 1)], vz_r.at[0])
    for i in range(nx):
        sums = vzs[z, i].astype(F32)
        for d in range(1, nz):
            sums = sums + vzr[(z + nz - d) % nz, i].astype(F32)
        vxs[i] = sums.astype(BF16)
    for d in range(nx):
        vx((d + 1) % nx).start()
    sum_x(SPLIT - 1)

    residual().wait_recv()
    for q in [*range(1, SPLIT - 1), 0, SPLIT - 1]:
        sums = finr[q].astype(F32)
        if q > 0:
            arrived(yzr.at[q], yz_r.at[q])
            for d in range(nz):
                sums = sums + yzr[q, (z + nz - d) % nz].astype(F32)
        else:
            arrived(vxr, vx_r.at[0])
            for d in range(nx):
                sums = sums + vxr[(x + nx - d) % nx].astype(F32)
        stage_o[...] = sums
        for j in range(8):
            start = q * wide + j * thin
            out[0, :, start : start + thin] = stage_o[2 * j : 2 * j + 2, :].astype(BF16)

    tail = pl.ds(1, SPLIT - 1)
    near_x = pl.ds(0, nx - 1)
    near_z = pl.ds(0, nz - 1)
    main = pl.ds(0, MAIN)
    rest = pl.ds(MAIN, HD - MAIN)
    left(hbuf.at[0, near_x], hx_s.at[0])
    left(hbuf.at[near_z], hz_s.at[0])
    left(gbuf.at[tail, near_z], az_s.at[0])
    left(xbuf.at[tail, 0, near_x], ax_s.at[0])
    left(xbuf.at[:, 0], ac_s.at[0])
    left(qbuf.at[near_z, 0, 0, main], qz_s.at[0])
    left(qbuf.at[:, 0, near_x, main], qx_s.at[0])
    left(qbuf.at[0, 0, near_x, rest], rx_s.at[0])
    left(qbuf.at[near_z, 0, :, rest], rz_s.at[0])
    left(qbuf.at[:, 0], qc_s.at[0])
    left(ocs, oc_s.at[0])
    left(lcs, lc_s.at[0])
    left(oxs.at[:, near_x], ox_s.at[0])
    left(lxs.at[:, near_x], lx_s.at[0])
    left(ozs.at[near_z], oz_s.at[0])
    left(lzs.at[near_z], lz_s.at[0])
    left(pzs.at[near_z], pz_s.at[0])
    left(mzs.at[near_z], mz_s.at[0])
    left(pxs.at[0, near_x], px_s.at[0])
    left(mxs.at[0, near_x], mx_s.at[0])
    left(ycs, yc_s.at[0])
    left(yxs.at[tail, near_x], yx_s.at[0])
    left(yzs.at[tail], yz_s.at[0])
    left(vzs.at[near_z], vz_s.at[0])
    left(vxs, vx_s.at[0])
    left(fin, sec_s.at[0])

    @pl.when(fresh_head == z)
    def _():
        left(fbuf.at[pl.ds(0, 2 * nx - 1)], f_s.at[0])

    @pl.when(fresh_head != z)
    def _():
        left(fbuf, f_s.at[0])


def local(n, nx, sections, hidden, norm_gain, w_query, w_kv, w_out, doc_cache, page_table, page_count):
    nz = n // (CORES * nx)
    span = 2 * n
    model = hidden.shape[-1]
    wide = model // SPLIT
    thin = wide // 8
    fresh_rows = w_kv.shape[-1]
    pages = doc_cache.shape[1]
    rest = HD - MAIN
    vmem = pl.BlockSpec(memory_space=pltpu.VMEM)
    smem = pl.BlockSpec(memory_space=pltpu.SMEM)
    anywhere = pl.BlockSpec(memory_space=pl.ANY)
    dma = pltpu.SemaphoreType.DMA

    def pair(waits):
        return [dma((1,)), dma((waits,))]

    scratch = [
        pltpu.VMEM((model, HD), BF16),
        pltpu.VMEM((fresh_rows, model), BF16),
        pltpu.VMEM((HD, model), BF16),
        pltpu.VMEM((2 * nz, pages, HD, HD), BF16),
        pltpu.VMEM((nz, HD, pages * HD), BF16),
        pltpu.VMEM((SPLIT, 16, thin), F32),
        pltpu.VMEM((SPLIT, 16, thin), F32),
        pltpu.VMEM((16, thin), F32),
        pltpu.VMEM((SPLIT, nz, 16, thin), BF16),
        pltpu.VMEM((nz, nx, 16, thin), BF16),
        pltpu.VMEM((SPLIT, CORES, nx, 2 * nz, wide), BF16),
        pltpu.VMEM((nz, CORES, nx, HD, span), BF16),
        pltpu.VMEM((fresh_rows, span), BF16),
        pltpu.VMEM((2 * nx, fresh_rows, span), BF16),
        pltpu.VMEM((nz, nx, HD, span), BF16),
        pltpu.VMEM((nz, nx, HD, span), BF16),
        pltpu.VMEM((nz, nx, 1, span), F32),
        pltpu.VMEM((nz, nx, 1, span), F32),
        pltpu.VMEM((PASS - 1, HD, nx * span), F32),
        pltpu.VMEM((PASS - 1, 1, nx * span), F32),
        pltpu.VMEM((nz, nx, MAIN, span), BF16),
        pltpu.VMEM((nz, nx, MAIN, span), BF16),
        pltpu.VMEM((nz, nx, 1, span), F32),
        pltpu.VMEM((nz, nx, 1, span), F32),
        pltpu.VMEM((nz, MAIN, span), BF16),
        pltpu.VMEM((nz, MAIN, span), BF16),
        pltpu.VMEM((nz, 1, span), F32),
        pltpu.VMEM((nz, 1, span), F32),
        pltpu.VMEM((nz, nx, rest, span), BF16),
        pltpu.VMEM((nz, nx, rest, span), BF16),
        pltpu.VMEM((nz, nx, 1, span), F32),
        pltpu.VMEM((nz, nx, 1, span), F32),
        pltpu.VMEM((1, nx, rest, span), BF16),
        pltpu.VMEM((1, nx, rest, span), BF16),
        pltpu.VMEM((1, nx, 1, span), F32),
        pltpu.VMEM((1, nx, 1, span), F32),
        pltpu.VMEM((CORES, span // CORES, HD), BF16),
        pltpu.VMEM((SPLIT, span // CORES, wide), BF16),
        pltpu.VMEM((SPLIT, span // CORES, wide), BF16),
        pltpu.VMEM((SPLIT, span // CORES, wide), F32),
        pltpu.VMEM((SPLIT, nx, 2 * nz, wide), BF16),
        pltpu.VMEM((SPLIT, nx, 2 * nz, wide), BF16),
        pltpu.VMEM((SPLIT, nz, 16, thin), BF16),
        pltpu.VMEM((SPLIT, nz, 16, thin), BF16),
        pltpu.VMEM((nz, nx, 16, thin), BF16),
        pltpu.VMEM((nz, nx, 16, thin), BF16),
        pltpu.VMEM((nx, 16, thin), BF16),
        pltpu.VMEM((nx, 16, thin), BF16),
        pltpu.VMEM((SPLIT, 16, thin), BF16),
        pltpu.VMEM((SPLIT, 16, thin), BF16),
        dma((3,)),
        dma((1,)),
        *pair(SPLIT),
        *pair(SPLIT),
        *pair(SPLIT),
        *pair(1),
        *pair(1),
        *pair(nz - 1),
        *pair(nz),
        *pair(nz),
        *pair(1),
        *pair(nz - 1),
        *pair(1),
        *pair(nz),
        *pair(nz),
        *pair(nz),
        *pair(nz),
        *pair(1),
        *pair(1),
        *pair(1),
        *pair(1),
        *pair(1),
        *pair(1),
        *pair(SPLIT),
        *pair(SPLIT),
        *pair(SPLIT),
        *pair(1),
        *pair(1),
        *pair(1),
    ]
    return pl.pallas_call(
        functools.partial(kernel, n, nz, nx, sections),
        out_shape=jax.ShapeDtypeStruct(hidden.shape, BF16),
        in_specs=[vmem, vmem, anywhere, anywhere, anywhere, anywhere, smem, smem],
        out_specs=vmem,
        scratch_shapes=scratch,
        compiler_params=pltpu.CompilerParams(
            collective_id=0, has_side_effects=True, vmem_limit_bytes=56 * 1024 * 1024
        ),
    )(hidden, norm_gain, w_query, jnp.swapaxes(w_kv, 1, 2), w_out, doc_cache, page_table, page_count)


def solution(mesh):
    placed = (
        P("section", "kvp", None),
        P("section", None),
        P("section", None, "kvp"),
        P("section", None, "kvp"),
        P("section", "kvp", None),
        P("section", "kvp", None, None),
        P("section", "kvp", None),
        P("section", "kvp"),
    )
    n = mesh.shape["kvp"]
    nx = RINGX if n >= 32 else 2
    return jax.shard_map(
        functools.partial(local, n, nx, mesh.shape["section"]),
        mesh=mesh,
        in_specs=placed,
        out_specs=P("section", "kvp", None),
        check_vma=False,
    )
```

time: 99.5 us -> 91 us (0.915)
  Pallas kernels: 96.4 us -> 88.4 us
    pallas_call x1, Pallas kernels: 96.4 us -> 88.4 us  [local(): pl.pallas_call(functools.partial(kernel, n, nz, nx, sections), out_shape=...]
where the time goes in v3:
time: 91 us; the launch traced here: 90.4 us
  Pallas kernels  88.4 us (97%)
  local copies, waits for them, and re-layouts  1.4 us (2%)
    pallas_call x1, Pallas kernels, local(): pl.pallas_call(functools.partial(kernel, n, nz, nx, sections), out_shape=...  88.4 us

profile of v3, /device:TPU:32, one launch (start us, length us, event | category | flops | bytes accessed | tf_op | source)
XLA Modules:
  0.0 90.4 jit_solution(5500108039827279261)
XLA Ops:
  0.7 88.4 %shard_map.82 = bf16[1,2,8192]{2,1,0:T(2,128)(2,1)} custom-call(bf16[1,2,8192]{2,1,0:T(2,128)(2,1)} %hid.1, bf16[1,8192]{1,0:T(2,128)(2,1)} %gain.1, bf16[1,8192,128]{2,1,0:T(8,128)(2,1)} %wq_hbm.1, bf16[1,32,8192]{2,1,0:T(8,128)(2,1)} %bitcast.1, bf16[1,128,8192]{2,1,0:T(8,128)(2,1)} %wout_hbm.1, bf16[1,4,128,2048]{3,2,1,0:T(8,128)(2,1)} %pool_hbm.1, ...), custom_call_target="tpu_custom_call" | custom-call | tf_op jit(solution)/shard_map/pallas_call | solution.py:824
  89.0 1.4 %copy.11 = bf16[1,2,8192]{2,1,0:T(2,128)(2,1)} copy(bf16[1,2,8192]{2,1,0:T(2,128)(2,1)} %shard_map.82) | data formatting | bytes 65536

commit v4 on v3

--- a/solution.py
+++ b/solution.py
@@ -20,9 +20,8 @@
 EPSILON = 1e-05
 BIG = 1e30
 LOG2E = 1.4426950408889634
-AHEAD = 3
-PASS = 3
-LAG = 8
+AHEAD = 5
+LAG = 6
 
 
 def dot(a, b, dims=((1,), (0,))):
@@ -73,6 +72,7 @@
     wout,
     kv,
     vt,
+    limits,
     stage_x,
     stage_n,
     stage_o,
@@ -82,12 +82,6 @@
     qbuf,
     fown,
     fbuf,
-    ocs,
-    ocr,
-    lcs,
-    lcr,
-    own_out,
-    own_level,
     oxs,
     oxr,
     lxs,
@@ -105,8 +99,7 @@
     mxs,
     mxr,
     att,
-    ycs,
-    ycr,
+    pair_att,
     yown,
     yxs,
     yxr,
@@ -120,6 +113,10 @@
     finr,
     load_sem,
     kv_sem,
+    kc_s,
+    kc_r,
+    bc_s,
+    bc_r,
     az_s,
     az_r,
     ax_s,
@@ -134,18 +131,12 @@
     qz_r,
     qx_s,
     qx_r,
-    qc_s,
-    qc_r,
     rx_s,
     rx_r,
     rz_s,
     rz_r,
     f_s,
     f_r,
-    oc_s,
-    oc_r,
-    lc_s,
-    lc_r,
     ox_s,
     ox_r,
     lx_s,
@@ -162,8 +153,10 @@
     px_r,
     mx_s,
     mx_r,
-    yc_s,
-    yc_r,
+    wc_s,
+    wc_r,
+    tc_s,
+    tc_r,
     yx_s,
     yx_r,
     yz_s,
@@ -213,6 +206,9 @@
     def left(region, sem):
         remote(region, region, sem, sem, peer).wait_send()
 
+    near_first = sorted(range(1, nz), key=lambda d: min(d, nz - d))
+    far_first = sorted(range(1, nz), key=lambda d: -min(d, nz - d))
+
     def to_z(d):
         return at((z + d) % nz, x, c)
 
@@ -222,10 +218,10 @@
     loads = [
         pltpu.make_async_copy(wq_hbm.at[0], wq, load_sem.at[0]),
         pltpu.make_async_copy(wkv_hbm.at[0], wkv, load_sem.at[1]),
-        pltpu.make_async_copy(wout_hbm.at[0], wout, load_sem.at[2]),
+        pltpu.make_async_copy(wout_hbm.at[0], wout.at[c], load_sem.at[2]),
     ]
     kv_loads = [
-        pltpu.make_async_copy(pool_hbm.at[0, :, :, pl.ds(i * HD, HD)], kv.at[i], kv_sem.at[0])
+        pltpu.make_async_copy(pool_hbm.at[0, :, :, pl.ds(i * HD, HD)], kv.at[c, i], kv_sem.at[0])
         for i in range(2 * kvh)
     ]
     for load in loads[:2] + kv_loads + loads[2:]:
@@ -291,19 +287,35 @@
     for d in range(1, nx):
         hx(d).start()
     for q in range(1, SPLIT):
-        for d in range(1, nz):
+        for d in far_first:
             az(q, d).start()
     arrived(hbuf.at[0, pl.ds(0, nx - 1)], hx_r.at[0])
-    for d in range(1, nz):
+    for d in far_first:
         hz(d).start()
     residual().start()
 
-    pltpu.make_async_copy(kv, kv, kv_sem.at[0]).wait()
-
-    @pl.loop(0, kvh)
-    def _(g):
-        vt[g] = kv[kvh + g].reshape(pages * HD, HD).T
-
+    row = lax.broadcasted_iota(jnp.int32, (8, span), 0)
+    bounds = jnp.zeros((8, span), F32)
+    for slot in range(pages):
+        bound = jnp.float32(BIG)
+        for j in range(pages):
+            named = jnp.logical_and(table[0, 0, j] == slot, j < count[0, 0])
+            bound = jnp.where(named, jnp.float32(-BIG), bound)
+        bounds = jnp.where(row == slot, bound, bounds)
+    limits[c] = bounds
+
+    pltpu.make_async_copy(kv.at[c], kv.at[c], kv_sem.at[0]).wait()
+    remote(kv.at[c], kv.at[c], kc_s.at[0], kc_r.at[0], peer).start()
+    remote(limits.at[c], limits.at[c], bc_s.at[0], bc_r.at[0], peer).start()
+    loads[2].wait()
+    remote(wout.at[c], wout.at[c], wc_s.at[0], wc_r.at[0], peer).start()
+
+    def transpose_values(core):
+        @pl.loop(0, kvh)
+        def _(g):
+            vt[core, g] = kv[core, kvh + g].reshape(pages * HD, HD).T
+
+    transpose_values(c)
     spread = row_order(16 * nz, nz, False)
     gather = row_order(16 * nz, nz, True)
     loads[0].wait()
@@ -329,6 +341,10 @@
                 for j in range(8):
                     xbuf[0, c, i, :, j * thin : (j + 1) * thin] = rows[j * 2 * nz : (j + 1) * 2 * nz]
             ac(0).start()
+        if t == 1:
+            arrived(kv.at[0], kc_r.at[0])
+            arrived(limits.at[0], bc_r.at[0])
+            transpose_values(1 - c)
         if 1 <= t <= SPLIT - 1:
             q = order[t - 1]
             arrived(xbuf.at[q, 0, pl.ds(0, nx - 1)], ax_r.at[q])
@@ -340,27 +356,24 @@
             query = query + dot(block, wq[q * wide : (q + 1) * wide])
             fresh = fresh + dot(wkv[:, q * wide : (q + 1) * wide], block, ((1,), (1,)))
 
-    qbuf[z, c, x] = query.T.astype(BF16)
+    qbuf[z, x] = query.T.astype(BF16)
     fown[...] = fresh.astype(BF16)
 
     def qz(d):
-        slot = qbuf.at[z, c, x, pl.ds(0, MAIN)]
+        slot = qbuf.at[z, x, pl.ds(0, MAIN)]
         return remote(slot, slot, qz_s.at[0], qz_r.at[d - 1], to_z(d))
 
     def qx(g, d):
-        slot = qbuf.at[g, c, x, pl.ds(0, MAIN)]
+        slot = qbuf.at[g, x, pl.ds(0, MAIN)]
         return remote(slot, slot, qx_s.at[0], qx_r.at[g], to_x(d))
 
     def rx(d):
-        slot = qbuf.at[z, c, x, pl.ds(MAIN, HD - MAIN)]
+        slot = qbuf.at[z, x, pl.ds(MAIN, HD - MAIN)]
         return remote(slot, slot, rx_s.at[0], rx_r.at[0], to_x(d))
 
     def rz(d):
-        slot = qbuf.at[z, c, :, pl.ds(MAIN, HD - MAIN)]
+        slot = qbuf.at[z, :, pl.ds(MAIN, HD - MAIN)]
         return remote(slot, slot, rz_s.at[0], rz_r.at[d - 1], to_z(d))
-
-    def qc(g):
-        return remote(qbuf.at[g, c], qbuf.at[g, c], qc_s.at[0], qc_r.at[g], peer)
 
     def fresh_out(i):
         return remote(
@@ -373,7 +386,7 @@
 
     for d in range(1, nx):
         rx(d).start()
-    for d in range(1, nz):
+    for d in near_first:
         qz(d).start()
     for d in range(1, nx):
         qx(z, d).start()
@@ -388,18 +401,14 @@
         def _():
             pltpu.make_async_copy(fown, fbuf.at[fresh_piece], f_r.at[0]).start()
 
-    bounds = []
-    for slot in range(pages):
-        bound = jnp.float32(BIG)
-        for j in range(pages):
-            named = jnp.logical_and(table[0, 0, j] == slot, j < count[0, 0])
-            bound = jnp.where(named, jnp.float32(-BIG), bound)
-        bounds.append(bound)
-
-    def attend(g, side):
-        cols = jnp.concatenate([qbuf[g, side, i] for i in range(nx)], axis=1)
-        scores = dot(kv[g].reshape(pages * HD, HD), cols)
-        parts = [scores[p * HD : (p + 1) * HD] for p in range(pages)]
+    def attend(g):
+        cols = jnp.concatenate([qbuf[g, i] for i in range(nx)], axis=1)
+        parts = []
+        bounds = []
+        for core in range(CORES):
+            scores = dot(kv[core, g].reshape(pages * HD, HD), cols)
+            parts += [scores[p * HD : (p + 1) * HD] for p in range(pages)]
+            bounds += [jnp.concatenate([limits[core, p : p + 1]] * nx, axis=1) for p in range(pages)]
         top = None
         for part, bound in zip(parts, bounds):
             here = jnp.minimum(jnp.max(part, axis=0, keepdims=True), -bound)
@@ -411,14 +420,12 @@
             add = jnp.sum(weight, axis=0, keepdims=True)
             total = add if total is None else total + add
             weights.append(weight.astype(BF16))
-        mixed = dot(vt[g], jnp.concatenate(weights, axis=0)) * (1.0 / total)
-        return mixed, top * scale + jnp.log(total) * LOG2E
-
-    def oc(g):
-        return remote(ocs.at[g], ocr.at[g], oc_s.at[0], oc_r.at[g], peer)
-
-    def lc(g):
-        return remote(lcs.at[g], lcr.at[g], lc_s.at[0], lc_r.at[g], peer)
+        mixed = None
+        for core in range(CORES):
+            here = jnp.concatenate(weights[core * pages : (core + 1) * pages], axis=0)
+            here = dot(vt[core, g], here)
+            mixed = here if mixed is None else mixed + here
+        return mixed * (1.0 / total), top * scale + jnp.log(total) * LOG2E
 
     def along_x(send, recv, send_sem, recv_sem):
         def out_copy(g, d):
@@ -449,73 +456,47 @@
     def forward(s):
         d = offset(s)
         g = (z + d) % nz
-        arrived(qbuf.at[g, 0, 0, pl.ds(0, MAIN)], qz_r.at[nz - d - 1])
+        arrived(qbuf.at[g, 0, pl.ds(0, MAIN)], qz_r.at[nz - d - 1])
         for e in range(1, nx):
             qx(g, e).start()
 
-    arrived(qbuf.at[0, 0, pl.ds(0, nx - 1), pl.ds(MAIN, HD - MAIN)], rx_r.at[0])
-    for d in range(1, nz):
+    arrived(qbuf.at[0, pl.ds(0, nx - 1), pl.ds(MAIN, HD - MAIN)], rx_r.at[0])
+    for d in near_first:
         rz(d).start()
     for s in range(1, min(AHEAD, nz)):
         forward(s)
 
     @pl.loop(0, nz + LAG)
     def _(t):
+        @pl.when(t < nz - AHEAD)
+        def _():
+            forward(t + AHEAD)
+
         @pl.when(t < nz)
         def _():
             d = offset(t)
             g = (z + d) % nz
-            arrived(qbuf.at[g, 0, pl.ds(0, nx - 1), pl.ds(0, MAIN)], qx_r.at[g])
+            arrived(qbuf.at[g, pl.ds(0, nx - 1), pl.ds(0, MAIN)], qx_r.at[g])
 
             @pl.when(t > 0)
             def _():
-                arrived(qbuf.at[g, 0, :, pl.ds(MAIN, HD - MAIN)], rz_r.at[nz - d - 1])
-
-            qc(g).start()
-
-        @pl.when(t < nz - AHEAD)
-        def _():
-            forward(t + AHEAD)
-
-        @pl.when(jnp.logical_and(t >= PASS, t < nz + PASS))
-        def _():
-            d = offset(t - PASS)
-            g = (z + d) % nz
-            slot = (t - PASS) % (PASS - 1)
-            arrived(ocr.at[g], oc_r.at[g])
-            arrived(lcr.at[g], lc_r.at[g])
+                arrived(qbuf.at[g, :, pl.ds(MAIN, HD - MAIN)], rz_r.at[nz - d - 1])
+
+            mixed, level = attend(g)
             for i in range(nx):
                 cols = slice(i * span, (i + 1) * span)
-                here = (own_out[slot, :, cols], own_level[slot, :, cols])
-                value, level = merge([here, (ocr[g, i].astype(F32), lcr[g, i])])
-                oxs[g, i] = value[:MAIN].astype(BF16)
-                lxs[g, i] = level
-                pzs[g, i] = value[MAIN:].astype(BF16)
-                mzs[g, i] = level
+                oxs[g, i] = mixed[:MAIN, cols].astype(BF16)
+                pzs[g, i] = mixed[MAIN:, cols].astype(BF16)
+                lxs[g, i] = level[:, cols]
+                mzs[g, i] = level[:, cols]
             for e in range(1, nx):
                 ox(g, e).start()
                 lx(g, e).start()
 
-            @pl.when(t > PASS)
+            @pl.when(t > 0)
             def _():
                 pz(g).start()
                 mz(g).start()
-
-        @pl.when(jnp.logical_and(t >= 1, t < nz + 1))
-        def _():
-            g = (z + offset(t - 1)) % nz
-            slot = (t - 1) % (PASS - 1)
-            arrived(qbuf.at[g, 0], qc_r.at[g])
-            mixed, level = attend(g, 1 - c)
-            for i in range(nx):
-                cols = slice(i * span, (i + 1) * span)
-                ocs[g, i] = mixed[:, cols].astype(BF16)
-                lcs[g, i] = level[:, cols]
-            oc(g).start()
-            lc(g).start()
-            mixed, level = attend(g, c)
-            own_out[slot] = mixed
-            own_level[slot] = level
 
         @pl.when(t >= LAG)
         def _():
@@ -563,7 +544,7 @@
         return ((tz * nx + tx) * CORES + tc) * 2 + r
 
     causal = token(0) <= token(1)
-    scores = dot(new_keys.T, qbuf[z, c, x])
+    scores = dot(new_keys.T, qbuf[z, x])
     scores = jnp.where(causal, scores, -BIG)
     top = jnp.max(scores, axis=0, keepdims=True)
     weights = jnp.where(causal, jnp.exp2((scores - top) * scale), 0.0)
@@ -586,11 +567,12 @@
     last_rows, _ = merge(parts)
     attention = jnp.concatenate([first_rows, last_rows], axis=0)
     att[...] = attention.T.astype(BF16).reshape(CORES, span // CORES, HD)
-
-    loads[2].wait()
-
-    def yc(q):
-        return remote(ycs.at[q], ycr.at[q], yc_s.at[0], yc_r.at[q], peer)
+    remote(att.at[1 - c], pair_att.at[c], tc_s.at[0], tc_r.at[0], peer).start()
+    pair_att[c] = att[c]
+    arrived(wout.at[0], wc_r.at[0])
+    arrived(pair_att.at[0], tc_r.at[0])
+    both = jnp.concatenate([pair_att[0], pair_att[1]], axis=1)
+
 
     def yx(q, d):
         return remote(
@@ -630,32 +612,24 @@
         for d in range(1, nx):
             sums = sums + yxr[q, (x + nx - d) % nx].astype(F32)
         yzs[q] = by_owner(sums.astype(BF16))
-        for d in range(nz):
-            yz(q, (d + 1) % nz).start()
-
-    for t in range(SPLIT + 1):
-        if t < SPLIT:
-            weight = wout[:, t * wide : (t + 1) * wide]
-            ycs[t] = dot(att[1 - c], weight).astype(BF16)
-            yc(t).start()
-            yown[t] = dot(att[c], weight)
-        if t >= 1:
-            q = t - 1
-            arrived(ycr.at[q], yc_r.at[q])
-            sums = yown[q] + ycr[q].astype(F32)
-            blocks = sums.astype(BF16).reshape(nx, 2 * nz, wide)
-            if q > 0:
-                yown[q] = sums
-                yxs[q] = blocks
-                for d in range(1, nx):
-                    yx(q, d).start()
-            else:
-                for i in range(nx):
-                    vzs[:, i] = by_owner(blocks[i])
-                for d in range(1, nz):
-                    vz(d).start()
-        if t >= 3:
-            sum_x(t - 2)
+        for d in [*far_first, 0]:
+            yz(q, d).start()
+
+    for q in range(SPLIT):
+        sums = dot(both, wout[:, :, q * wide : (q + 1) * wide].reshape(CORES * HD, wide))
+        blocks = sums.astype(BF16).reshape(nx, 2 * nz, wide)
+        if q > 0:
+            yown[q] = sums
+            yxs[q] = blocks
+            for d in range(1, nx):
+                yx(q, d).start()
+        else:
+            for i in range(nx):
+                vzs[:, i] = by_owner(blocks[i])
+            for d in far_first:
+                vz(d).start()
+    for q in range(1, SPLIT - 1):
+        sum_x(q)
     arrived(vzr.at[pl.ds(0, nz - 1)], vz_r.at[0])
     for i in range(nx):
         sums = vzs[z, i].astype(F32)
@@ -692,13 +666,12 @@
     left(gbuf.at[tail, near_z], az_s.at[0])
     left(xbuf.at[tail, 0, near_x], ax_s.at[0])
     left(xbuf.at[:, 0], ac_s.at[0])
-    left(qbuf.at[near_z, 0, 0, main], qz_s.at[0])
-    left(qbuf.at[:, 0, near_x, main], qx_s.at[0])
-    left(qbuf.at[0, 0, near_x, rest], rx_s.at[0])
-    left(qbuf.at[near_z, 0, :, rest], rz_s.at[0])
-    left(qbuf.at[:, 0], qc_s.at[0])
-    left(ocs, oc_s.at[0])
-    left(lcs, lc_s.at[0])
+    left(kv.at[0], kc_s.at[0])
+    left(limits.at[0], bc_s.at[0])
+    left(qbuf.at[near_z, 0, main], qz_s.at[0])
+    left(qbuf.at[:, near_x, main], qx_s.at[0])
+    left(qbuf.at[0, near_x, rest], rx_s.at[0])
+    left(qbuf.at[near_z, :, rest], rz_s.at[0])
     left(oxs.at[:, near_x], ox_s.at[0])
     left(lxs.at[:, near_x], lx_s.at[0])
     left(ozs.at[near_z], oz_s.at[0])
@@ -707,7 +680,8 @@
     left(mzs.at[near_z], mz_s.at[0])
     left(pxs.at[0, near_x], px_s.at[0])
     left(mxs.at[0, near_x], mx_s.at[0])
-    left(ycs, yc_s.at[0])
+    left(wout.at[0], wc_s.at[0])
+    left(att.at[0], tc_s.at[0])
     left(yxs.at[tail, near_x], yx_s.at[0])
     left(yzs.at[tail], yz_s.at[0])
     left(vzs.at[near_z], vz_s.at[0])
@@ -743,24 +717,19 @@
     scratch = [
         pltpu.VMEM((model, HD), BF16),
         pltpu.VMEM((fresh_rows, model), BF16),
-        pltpu.VMEM((HD, model), BF16),
-        pltpu.VMEM((2 * nz, pages, HD, HD), BF16),
-        pltpu.VMEM((nz, HD, pages * HD), BF16),
+        pltpu.VMEM((CORES, HD, model), BF16),
+        pltpu.VMEM((CORES, 2 * nz, pages, HD, HD), BF16),
+        pltpu.VMEM((CORES, nz, HD, pages * HD), BF16),
+        pltpu.VMEM((CORES, 8, span), F32),
         pltpu.VMEM((SPLIT, 16, thin), F32),
         pltpu.VMEM((SPLIT, 16, thin), F32),
         pltpu.VMEM((16, thin), F32),
         pltpu.VMEM((SPLIT, nz, 16, thin), BF16),
         pltpu.VMEM((nz, nx, 16, thin), BF16),
         pltpu.VMEM((SPLIT, CORES, nx, 2 * nz, wide), BF16),
-        pltpu.VMEM((nz, CORES, nx, HD, span), BF16),
+        pltpu.VMEM((nz, nx, HD, span), BF16),
         pltpu.VMEM((fresh_rows, span), BF16),
         pltpu.VMEM((2 * nx, fresh_rows, span), BF16),
-        pltpu.VMEM((nz, nx, HD, span), BF16),
-        pltpu.VMEM((nz, nx, HD, span), BF16),
-        pltpu.VMEM((nz, nx, 1, span), F32),
-        pltpu.VMEM((nz, nx, 1, span), F32),
-        pltpu.VMEM((PASS - 1, HD, nx * span), F32),
-        pltpu.VMEM((PASS - 1, 1, nx * span), F32),
         pltpu.VMEM((nz, nx, MAIN, span), BF16),
         pltpu.VMEM((nz, nx, MAIN, span), BF16),
         pltpu.VMEM((nz, nx, 1, span), F32),
@@ -778,8 +747,7 @@
         pltpu.VMEM((1, nx, 1, span), F32),
         pltpu.VMEM((1, nx, 1, span), F32),
         pltpu.VMEM((CORES, span // CORES, HD), BF16),
-        pltpu.VMEM((SPLIT, span // CORES, wide), BF16),
-        pltpu.VMEM((SPLIT, span // CORES, wide), BF16),
+        pltpu.VMEM((CORES, span // CORES, HD), BF16),
         pltpu.VMEM((SPLIT, span // CORES, wide), F32),
         pltpu.VMEM((SPLIT, nx, 2 * nz, wide), BF16),
         pltpu.VMEM((SPLIT, nx, 2 * nz, wide), BF16),
@@ -793,6 +761,8 @@
         pltpu.VMEM((SPLIT, 16, thin), BF16),
         dma((3,)),
         dma((1,)),
+        *pair(1),
+        *pair(1),
         *pair(SPLIT),
         *pair(SPLIT),
         *pair(SPLIT),
@@ -800,21 +770,19 @@
         *pair(1),
         *pair(nz - 1),
         *pair(nz),
-        *pair(nz),
         *pair(1),
         *pair(nz - 1),
         *pair(1),
         *pair(nz),
         *pair(nz),
-        *pair(nz),
-        *pair(nz),
-        *pair(1),
-        *pair(1),
-        *pair(1),
-        *pair(1),
-        *pair(1),
-        *pair(1),
-        *pair(SPLIT),
+        *pair(1),
+        *pair(1),
+        *pair(1),
+        *pair(1),
+        *pair(1),
+        *pair(1),
+        *pair(1),
+        *pair(1),
         *pair(SPLIT),
         *pair(SPLIT),
         *pair(1),

time: 91 us -> 81.8 us (0.90)
  Pallas kernels: 88.4 us -> 78.7 us
    pallas_call x1, Pallas kernels: 88.4 us -> 78.7 us  [local(): pl.pallas_call(functools.partial(kernel, n, nz, nx, sections), out_shape=...]
where the time goes in v4:
time: 81.8 us; the launch traced here: 80.8 us
  Pallas kernels  78.7 us (96%)
  local copies, waits for them, and re-layouts  1.4 us (2%)
    pallas_call x1, Pallas kernels, local(): pl.pallas_call(functools.partial(kernel, n, nz, nx, sections), out_shape=...  78.7 us

profile of v4, /device:TPU:32, one launch (start us, length us, event | category | flops | bytes accessed | tf_op | source)
XLA Modules:
  0.0 80.8 jit_solution(8836929723973802155)
XLA Ops:
  0.7 78.7 %shard_map.82 = bf16[1,2,8192]{2,1,0:T(2,128)(2,1)} custom-call(bf16[1,2,8192]{2,1,0:T(2,128)(2,1)} %hid.1, bf16[1,8192]{1,0:T(2,128)(2,1)} %gain.1, bf16[1,8192,128]{2,1,0:T(8,128)(2,1)} %wq_hbm.1, bf16[1,32,8192]{2,1,0:T(8,128)(2,1)} %bitcast.1, bf16[1,128,8192]{2,1,0:T(8,128)(2,1)} %wout_hbm.1, bf16[1,4,128,2048]{3,2,1,0:T(8,128)(2,1)} %pool_hbm.1, ...), custom_call_target="tpu_custom_call" | custom-call | tf_op jit(solution)/shard_map/pallas_call | solution.py:792
  79.4 1.4 %copy.11 = bf16[1,2,8192]{2,1,0:T(2,128)(2,1)} copy(bf16[1,2,8192]{2,1,0:T(2,128)(2,1)} %shard_map.82) | data formatting | bytes 65536

commit v5 on v4

--- a/solution.py
+++ b/solution.py
@@ -80,6 +80,8 @@
     hbuf,
     xbuf,
     qbuf,
+    fpair,
+    fturn,
     fown,
     fbuf,
     oxs,
@@ -98,8 +100,6 @@
     pxr,
     mxs,
     mxr,
-    att,
-    pair_att,
     yown,
     yxs,
     yxr,
@@ -121,8 +121,12 @@
     az_r,
     ax_s,
     ax_r,
-    ac_s,
-    ac_r,
+    dc_s,
+    dc_r,
+    ec_s,
+    ec_r,
+    fc_s,
+    fc_r,
     hx_s,
     hx_r,
     hz_s,
@@ -155,8 +159,6 @@
     mx_r,
     wc_s,
     wc_r,
-    tc_s,
-    tc_r,
     yx_s,
     yx_r,
     yz_s,
@@ -170,6 +172,7 @@
 ):
     kvh = nz
     span = 2 * n
+    half_span = span // CORES
     model = hid.shape[-1]
     wide = model // SPLIT
     thin = wide // 8
@@ -216,8 +219,8 @@
         return at(z, (x + d) % nx, c)
 
     loads = [
-        pltpu.make_async_copy(wq_hbm.at[0], wq, load_sem.at[0]),
-        pltpu.make_async_copy(wkv_hbm.at[0], wkv, load_sem.at[1]),
+        pltpu.make_async_copy(wq_hbm.at[0], wq.at[c], load_sem.at[0]),
+        pltpu.make_async_copy(wkv_hbm.at[0], wkv.at[c], load_sem.at[1]),
         pltpu.make_async_copy(wout_hbm.at[0], wout.at[c], load_sem.at[2]),
     ]
     kv_loads = [
@@ -272,11 +275,8 @@
         return remote(gbuf.at[q, z], gbuf.at[q, z], az_s.at[0], az_r.at[q], to_z(d))
 
     def ax(q, d):
-        slot = xbuf.at[q, c, x]
+        slot = xbuf.at[q, x]
         return remote(slot, slot, ax_s.at[0], ax_r.at[q], to_x(d))
-
-    def ac(q):
-        return remote(xbuf.at[q, c], xbuf.at[q, c], ac_s.at[0], ac_r.at[q], peer)
 
     def hx(d):
         return remote(hbuf.at[z, x], hbuf.at[z, x], hx_s.at[0], hx_r.at[0], to_x(d))
@@ -304,6 +304,12 @@
         bounds = jnp.where(row == slot, bound, bounds)
     limits[c] = bounds
 
+    if wkv.shape[0] > CORES:
+        wkv[CORES:] = jnp.zeros((wkv.shape[0] - CORES, *wkv.shape[1:]), BF16)
+    loads[0].wait()
+    remote(wq.at[c], wq.at[c], dc_s.at[0], dc_r.at[0], peer).start()
+    loads[1].wait()
+    remote(wkv.at[c], wkv.at[c], ec_s.at[0], ec_r.at[0], peer).start()
     pltpu.make_async_copy(kv.at[c], kv.at[c], kv_sem.at[0]).wait()
     remote(kv.at[c], kv.at[c], kc_s.at[0], kc_r.at[0], peer).start()
     remote(limits.at[c], limits.at[c], bc_s.at[0], bc_r.at[0], peer).start()
@@ -318,19 +324,17 @@
     transpose_values(c)
     spread = row_order(16 * nz, nz, False)
     gather = row_order(16 * nz, nz, True)
-    loads[0].wait()
-    loads[1].wait()
-
-    query = jnp.zeros((span, HD), F32)
-    fresh = jnp.zeros((wkv.shape[0], span), F32)
+
+    queries = [jnp.zeros((half_span, HD), F32) for _ in range(CORES)]
+    fresh = jnp.zeros((half_span, HD), F32)
     order = [*range(1, SPLIT), 0]
-    for t in range(SPLIT + 2):
+    for t in range(SPLIT + 1):
         if t < SPLIT - 1:
             q = order[t]
             arrived(gbuf.at[q, pl.ds(0, nz - 1)], az_r.at[q])
             rows = dot(spread, gbuf[q].reshape(16 * nz, thin)).astype(BF16)
             for j in range(8):
-                xbuf[q, c, x, :, j * thin : (j + 1) * thin] = rows[j * 2 * nz : (j + 1) * 2 * nz]
+                xbuf[q, x, :, j * thin : (j + 1) * thin] = rows[j * 2 * nz : (j + 1) * 2 * nz]
             for d in range(1, nx):
                 ax(q, d).start()
         elif t == SPLIT - 1:
@@ -339,25 +343,25 @@
                 block = jnp.concatenate([hbuf[k, i] for k in range(nz)], axis=0)
                 rows = dot(spread, block).astype(BF16)
                 for j in range(8):
-                    xbuf[0, c, i, :, j * thin : (j + 1) * thin] = rows[j * 2 * nz : (j + 1) * 2 * nz]
-            ac(0).start()
+                    xbuf[0, i, :, j * thin : (j + 1) * thin] = rows[j * 2 * nz : (j + 1) * 2 * nz]
         if t == 1:
             arrived(kv.at[0], kc_r.at[0])
             arrived(limits.at[0], bc_r.at[0])
             transpose_values(1 - c)
-        if 1 <= t <= SPLIT - 1:
+            arrived(wq.at[0], dc_r.at[0])
+            arrived(wkv.at[0], ec_r.at[0])
+        if t >= 1:
             q = order[t - 1]
-            arrived(xbuf.at[q, 0, pl.ds(0, nx - 1)], ax_r.at[q])
-            ac(q).start()
-        if t >= 2:
-            q = order[t - 2]
-            arrived(xbuf.at[q, 0], ac_r.at[q])
-            block = xbuf[q].reshape(span, wide)
-            query = query + dot(block, wq[q * wide : (q + 1) * wide])
-            fresh = fresh + dot(wkv[:, q * wide : (q + 1) * wide], block, ((1,), (1,)))
-
-    qbuf[z, x] = query.T.astype(BF16)
-    fown[...] = fresh.astype(BF16)
+            if q > 0:
+                arrived(xbuf.at[q, pl.ds(0, nx - 1)], ax_r.at[q])
+            block = xbuf[q].reshape(half_span, wide)
+            cols = slice(q * wide, (q + 1) * wide)
+            queries = [queries[h] + dot(block, wq[h, cols]) for h in range(CORES)]
+            fresh = fresh + dot(block, wkv[:, :, cols].reshape(HD, wide), ((1,), (1,)))
+
+    qbuf[z, x] = jnp.concatenate(queries, axis=0).T.astype(BF16)
+    fpair[c] = fresh.astype(BF16)
+    remote(fpair.at[c], fpair.at[c], fc_s.at[0], fc_r.at[0], peer).start()
 
     def qz(d):
         slot = qbuf.at[z, x, pl.ds(0, MAIN)]
@@ -390,17 +394,6 @@
         qz(d).start()
     for d in range(1, nx):
         qx(z, d).start()
-    for i in range(2 * nx):
-        target = fresh_head * CORES * nx + i
-
-        @pl.when(target != me)
-        def _():
-            fresh_out(i).start()
-
-        @pl.when(target == me)
-        def _():
-            pltpu.make_async_copy(fown, fbuf.at[fresh_piece], f_r.at[0]).start()
-
     def attend(g):
         cols = jnp.concatenate([qbuf[g, i] for i in range(nx)], axis=1)
         parts = []
@@ -466,6 +459,20 @@
     for s in range(1, min(AHEAD, nz)):
         forward(s)
 
+    arrived(fpair.at[0], fc_r.at[0])
+    fturn[...] = fpair[...].astype(F32).reshape(span, HD).T.astype(BF16).reshape(fturn.shape)
+    fown[...] = fturn[c]
+    for i in range(2 * nx):
+        target = fresh_head * CORES * nx + i
+
+        @pl.when(target != me)
+        def _():
+            fresh_out(i).start()
+
+        @pl.when(target == me)
+        def _():
+            pltpu.make_async_copy(fown, fbuf.at[fresh_piece], f_r.at[0]).start()
+
     @pl.loop(0, nz + LAG)
     def _(t):
         @pl.when(t < nz - AHEAD)
@@ -535,15 +542,16 @@
     new_keys = fbuf[:nx].reshape(HD, span)
     new_values = fbuf[nx:].reshape(HD, span)
 
-    def token(axis):
-        row = lax.broadcasted_iota(jnp.int32, (span, span), axis)
+    def token(row):
         r = row % 2
         tz = (row // 2) % nz
         tx = (row // (2 * nz)) % nx
         tc = row // (2 * nz * nx)
         return ((tz * nx + tx) * CORES + tc) * 2 + r
 
-    causal = token(0) <= token(1)
+    key_row = lax.broadcasted_iota(jnp.int32, (span, span), 0)
+    query_lane = lax.broadcasted_iota(jnp.int32, (span, span), 1)
+    causal = token(key_row) <= token(c * half_span + query_lane % half_span)
     scores = dot(new_keys.T, qbuf[z, x])
     scores = jnp.where(causal, scores, -BIG)
     top = jnp.max(scores, axis=0, keepdims=True)
@@ -566,12 +574,9 @@
         parts.append((pxr[0, slot].astype(F32), mxr[0, slot]))
     last_rows, _ = merge(parts)
     attention = jnp.concatenate([first_rows, last_rows], axis=0)
-    att[...] = attention.T.astype(BF16).reshape(CORES, span // CORES, HD)
-    remote(att.at[1 - c], pair_att.at[c], tc_s.at[0], tc_r.at[0], peer).start()
-    pair_att[c] = att[c]
+    attention = attention.T.astype(BF16)
+    both = jnp.concatenate([attention[:half_span], attention[half_span:]], axis=1)
     arrived(wout.at[0], wc_r.at[0])
-    arrived(pair_att.at[0], tc_r.at[0])
-    both = jnp.concatenate([pair_att[0], pair_att[1]], axis=1)
 
 
     def yx(q, d):
@@ -664,8 +669,10 @@
     left(hbuf.at[0, near_x], hx_s.at[0])
     left(hbuf.at[near_z], hz_s.at[0])
     left(gbuf.at[tail, near_z], az_s.at[0])
-    left(xbuf.at[tail, 0, near_x], ax_s.at[0])
-    left(xbuf.at[:, 0], ac_s.at[0])
+    left(xbuf.at[tail, near_x], ax_s.at[0])
+    left(wq.at[0], dc_s.at[0])
+    left(wkv.at[0], ec_s.at[0])
+    left(fpair.at[0], fc_s.at[0])
     left(kv.at[0], kc_s.at[0])
     left(limits.at[0], bc_s.at[0])
     left(qbuf.at[near_z, 0, main], qz_s.at[0])
@@ -681,7 +688,6 @@
     left(pxs.at[0, near_x], px_s.at[0])
     left(mxs.at[0, near_x], mx_s.at[0])
     left(wout.at[0], wc_s.at[0])
-    left(att.at[0], tc_s.at[0])
     left(yxs.at[tail, near_x], yx_s.at[0])
     left(yzs.at[tail], yz_s.at[0])
     left(vzs.at[near_z], vz_s.at[0])
@@ -715,8 +721,8 @@
         return [dma((1,)), dma((waits,))]
 
     scratch = [
-        pltpu.VMEM((model, HD), BF16),
-        pltpu.VMEM((fresh_rows, model), BF16),
+        pltpu.VMEM((CORES, model, HD), BF16),
+        pltpu.VMEM((nx, fresh_rows, model), BF16),
         pltpu.VMEM((CORES, HD, model), BF16),
         pltpu.VMEM((CORES, 2 * nz, pages, HD, HD), BF16),
         pltpu.VMEM((CORES, nz, HD, pages * HD), BF16),
@@ -726,8 +732,10 @@
         pltpu.VMEM((16, thin), F32),
         pltpu.VMEM((SPLIT, nz, 16, thin), BF16),
         pltpu.VMEM((nz, nx, 16, thin), BF16),
-        pltpu.VMEM((SPLIT, CORES, nx, 2 * nz, wide), BF16),
+        pltpu.VMEM((SPLIT, nx, 2 * nz, wide), BF16),
         pltpu.VMEM((nz, nx, HD, span), BF16),
+        pltpu.VMEM((CORES, span // CORES, HD), BF16),
+        pltpu.VMEM((nx, fresh_rows, span), BF16),
         pltpu.VMEM((fresh_rows, span), BF16),
         pltpu.VMEM((2 * nx, fresh_rows, span), BF16),
         pltpu.VMEM((nz, nx, MAIN, span), BF16),
@@ -746,8 +754,6 @@
         pltpu.VMEM((1, nx, rest, span), BF16),
         pltpu.VMEM((1, nx, 1, span), F32),
         pltpu.VMEM((1, nx, 1, span), F32),
-        pltpu.VMEM((CORES, span // CORES, HD), BF16),
-        pltpu.VMEM((CORES, span // CORES, HD), BF16),
         pltpu.VMEM((SPLIT, span // CORES, wide), F32),
         pltpu.VMEM((SPLIT, nx, 2 * nz, wide), BF16),
         pltpu.VMEM((SPLIT, nx, 2 * nz, wide), BF16),
@@ -765,7 +771,9 @@
         *pair(1),
         *pair(SPLIT),
         *pair(SPLIT),
-        *pair(SPLIT),
+        *pair(1),
+        *pair(1),
+        *pair(1),
         *pair(1),
         *pair(1),
         *pair(nz - 1),
@@ -775,7 +783,6 @@
         *pair(1),
         *pair(nz),
         *pair(nz),
-        *pair(1),
         *pair(1),
         *pair(1),
         *pair(1),

time: 81.8 us -> 76.4 us (0.934)
  Pallas kernels: 78.7 us -> 74.1 us
    pallas_call x1, Pallas kernels: 78.7 us -> 74.1 us  [local(): pl.pallas_call(functools.partial(kernel, n, nz, nx, sections), out_shape=...]
where the time goes in v5:
time: 76.4 us; the launch traced here: 76.2 us
  Pallas kernels  74.1 us (97%)
  local copies, waits for them, and re-layouts  1.4 us (2%)
    pallas_call x1, Pallas kernels, local(): pl.pallas_call(functools.partial(kernel, n, nz, nx, sections), out_shape=...  74.1 us

profile of v5, /device:TPU:32, one launch (start us, length us, event | category | flops | bytes accessed | tf_op | source)
XLA Modules:
  0.0 76.2 jit_solution(15020850639750982540)
XLA Ops:
  0.7 74.1 %shard_map.82 = bf16[1,2,8192]{2,1,0:T(2,128)(2,1)} custom-call(bf16[1,2,8192]{2,1,0:T(2,128)(2,1)} %hid.1, bf16[1,8192]{1,0:T(2,128)(2,1)} %gain.1, bf16[1,8192,128]{2,1,0:T(8,128)(2,1)} %wq_hbm.1, bf16[1,32,8192]{2,1,0:T(8,128)(2,1)} %bitcast.1, bf16[1,128,8192]{2,1,0:T(8,128)(2,1)} %wout_hbm.1, bf16[1,4,128,2048]{3,2,1,0:T(8,128)(2,1)} %pool_hbm.1, ...), custom_call_target="tpu_custom_call" | custom-call | tf_op jit(solution)/shard_map/pallas_call | solution.py:799
  74.8 1.4 %copy.11 = bf16[1,2,8192]{2,1,0:T(2,128)(2,1)} copy(bf16[1,2,8192]{2,1,0:T(2,128)(2,1)} %shard_map.82) | data formatting | bytes 65536

commit v6 on v5

--- a/solution.py
+++ b/solution.py
@@ -209,6 +209,7 @@
     def left(region, sem):
         remote(region, region, sem, sem, peer).wait_send()
 
+    across = sorted(range(1, nx), key=lambda d: -min(d, nx - d))
     near_first = sorted(range(1, nz), key=lambda d: min(d, nz - d))
     far_first = sorted(range(1, nz), key=lambda d: -min(d, nz - d))
 
@@ -335,7 +336,7 @@
             rows = dot(spread, gbuf[q].reshape(16 * nz, thin)).astype(BF16)
             for j in range(8):
                 xbuf[q, x, :, j * thin : (j + 1) * thin] = rows[j * 2 * nz : (j + 1) * 2 * nz]
-            for d in range(1, nx):
+            for d in across:
                 ax(q, d).start()
         elif t == SPLIT - 1:
             arrived(hbuf.at[pl.ds(0, nz - 1)], hz_r.at[0])
@@ -450,7 +451,7 @@
         d = offset(s)
         g = (z + d) % nz
         arrived(qbuf.at[g, 0, pl.ds(0, MAIN)], qz_r.at[nz - d - 1])
-        for e in range(1, nx):
+        for e in across:
             qx(g, e).start()
 
     arrived(qbuf.at[0, pl.ds(0, nx - 1), pl.ds(MAIN, HD - MAIN)], rx_r.at[0])
@@ -458,20 +459,6 @@
         rz(d).start()
     for s in range(1, min(AHEAD, nz)):
         forward(s)
-
-    arrived(fpair.at[0], fc_r.at[0])
-    fturn[...] = fpair[...].astype(F32).reshape(span, HD).T.astype(BF16).reshape(fturn.shape)
-    fown[...] = fturn[c]
-    for i in range(2 * nx):
-        target = fresh_head * CORES * nx + i
-
-        @pl.when(target != me)
-        def _():
-            fresh_out(i).start()
-
-        @pl.when(target == me)
-        def _():
-            pltpu.make_async_copy(fown, fbuf.at[fresh_piece], f_r.at[0]).start()
 
     @pl.loop(0, nz + LAG)
     def _(t):
@@ -496,14 +483,32 @@
                 pzs[g, i] = mixed[MAIN:, cols].astype(BF16)
                 lxs[g, i] = level[:, cols]
                 mzs[g, i] = level[:, cols]
-            for e in range(1, nx):
+            for e in across:
+                lx(g, e).start()
+            for e in across:
                 ox(g, e).start()
-                lx(g, e).start()
 
             @pl.when(t > 0)
             def _():
+                mz(g).start()
                 pz(g).start()
-                mz(g).start()
+
+        @pl.when(t == 1)
+        def _():
+            arrived(fpair.at[0], fc_r.at[0])
+            fturn[...] = fpair[...].astype(F32).reshape(span, HD).T.astype(BF16).reshape(fturn.shape)
+            fown[...] = fturn[c]
+            for i in range(2 * nx):
+                target = fresh_head * CORES * nx + i
+
+                @pl.when(target != me)
+                def _():
+                    fresh_out(i).start()
+
+                @pl.when(target == me)
+                def _():
+                    pltpu.make_async_copy(fown, fbuf.at[fresh_piece], f_r.at[0]).start()
+
 
         @pl.when(t >= LAG)
         def _():
@@ -521,8 +526,8 @@
 
             @pl.when(t > LAG)
             def _():
+                lz(g).start()
                 oz(g).start()
-                lz(g).start()
 
     pz_in()
     mz_in()
@@ -620,13 +625,13 @@
         for d in [*far_first, 0]:
             yz(q, d).start()
 
-    for q in range(SPLIT):
+    for q in [1, 0, *range(2, SPLIT)]:
         sums = dot(both, wout[:, :, q * wide : (q + 1) * wide].reshape(CORES * HD, wide))
         blocks = sums.astype(BF16).reshape(nx, 2 * nz, wide)
         if q > 0:
             yown[q] = sums
             yxs[q] = blocks
-            for d in range(1, nx):
+            for d in across:
                 yx(q, d).start()
         else:
             for i in range(nx):

time: 76.4 us -> 74.7 us (0.978)
  Pallas kernels: 74.1 us -> 72.1 us
    pallas_call x1, Pallas kernels: 74.1 us -> 72.1 us  [local(): pl.pallas_call(functools.partial(kernel, n, nz, nx, sections), out_shape=...]
where the time goes in v6:
time: 74.7 us; the launch traced here: 74.1 us
  Pallas kernels  72.1 us (97%)
  local copies, waits for them, and re-layouts  1.4 us (2%)
    pallas_call x1, Pallas kernels, local(): pl.pallas_call(functools.partial(kernel, n, nz, nx, sections), out_shape=...  72.1 us

profile of v6, /device:TPU:32, one launch (start us, length us, event | category | flops | bytes accessed | tf_op | source)
XLA Modules:
  0.0 74.1 jit_solution(535933851647811161)
XLA Ops:
  0.7 72.1 %shard_map.82 = bf16[1,2,8192]{2,1,0:T(2,128)(2,1)} custom-call(bf16[1,2,8192]{2,1,0:T(2,128)(2,1)} %hid.1, bf16[1,8192]{1,0:T(2,128)(2,1)} %gain.1, bf16[1,8192,128]{2,1,0:T(8,128)(2,1)} %wq_hbm.1, bf16[1,32,8192]{2,1,0:T(8,128)(2,1)} %bitcast.1, bf16[1,128,8192]{2,1,0:T(8,128)(2,1)} %wout_hbm.1, bf16[1,4,128,2048]{3,2,1,0:T(8,128)(2,1)} %pool_hbm.1, ...), custom_call_target="tpu_custom_call" | custom-call | tf_op jit(solution)/shard_map/pallas_call | solution.py:804
  72.7 1.4 %copy.11 = bf16[1,2,8192]{2,1,0:T(2,128)(2,1)} copy(bf16[1,2,8192]{2,1,0:T(2,128)(2,1)} %shard_map.82) | data formatting | bytes 65536

commit v7 on v6

--- a/solution.py
+++ b/solution.py
@@ -285,14 +285,11 @@
     def hz(d):
         return remote(hbuf.at[z], hbuf.at[z], hz_s.at[0], hz_r.at[0], to_z(d))
 
-    for d in range(1, nx):
+    for d in across:
         hx(d).start()
     for q in range(1, SPLIT):
         for d in far_first:
             az(q, d).start()
-    arrived(hbuf.at[0, pl.ds(0, nx - 1)], hx_r.at[0])
-    for d in far_first:
-        hz(d).start()
     residual().start()
 
     row = lax.broadcasted_iota(jnp.int32, (8, span), 0)
@@ -322,6 +319,9 @@
         def _(g):
             vt[core, g] = kv[core, kvh + g].reshape(pages * HD, HD).T
 
+    arrived(hbuf.at[0, pl.ds(0, nx - 1)], hx_r.at[0])
+    for d in far_first:
+        hz(d).start()
     transpose_values(c)
     spread = row_order(16 * nz, nz, False)
     gather = row_order(16 * nz, nz, True)
@@ -389,11 +389,11 @@
             fresh_head * CORES * nx + i,
         )
 
-    for d in range(1, nx):
+    for d in across:
         rx(d).start()
     for d in near_first:
         qz(d).start()
-    for d in range(1, nx):
+    for d in across:
         qx(z, d).start()
     def attend(g):
         cols = jnp.concatenate([qbuf[g, i] for i in range(nx)], axis=1)
@@ -539,9 +539,9 @@
         value, level = merge(parts)
         pxs[0, i] = value.astype(BF16)
         mxs[0, i] = level
-    for e in range(1, nx):
+    for e in across:
+        mx(0, e).start()
         px(0, e).start()
-        mx(0, e).start()
 
     arrived(fbuf, f_r.at[0])
     new_keys = fbuf[:nx].reshape(HD, span)

time: 74.7 us -> 70.7 us (0.946)
  Pallas kernels: 72.1 us -> 68.3 us
    pallas_call x1, Pallas kernels: 72.1 us -> 68.3 us  [local(): pl.pallas_call(functools.partial(kernel, n, nz, nx, sections), out_shape=...]
where the time goes in v7:
time: 70.7 us; the launch traced here: 70.4 us
  Pallas kernels  68.3 us (97%)
  local copies, waits for them, and re-layouts  1.4 us (2%)
    pallas_call x1, Pallas kernels, local(): pl.pallas_call(functools.partial(kernel, n, nz, nx, sections), out_shape=...  68.3 us

profile of v7, /device:TPU:32, one launch (start us, length us, event | category | flops | bytes accessed | tf_op | source)
XLA Modules:
  0.0 70.4 jit_solution(4592676260244491467)
XLA Ops:
  0.7 68.3 %shard_map.82 = bf16[1,2,8192]{2,1,0:T(2,128)(2,1)} custom-call(bf16[1,2,8192]{2,1,0:T(2,128)(2,1)} %hid.1, bf16[1,8192]{1,0:T(2,128)(2,1)} %gain.1, bf16[1,8192,128]{2,1,0:T(8,128)(2,1)} %wq_hbm.1, bf16[1,32,8192]{2,1,0:T(8,128)(2,1)} %bitcast.1, bf16[1,128,8192]{2,1,0:T(8,128)(2,1)} %wout_hbm.1, bf16[1,4,128,2048]{3,2,1,0:T(8,128)(2,1)} %pool_hbm.1, ...), custom_call_target="tpu_custom_call" | custom-call | tf_op jit(solution)/shard_map/pallas_call | solution.py:804
  69.0 1.4 %copy.11 = bf16[1,2,8192]{2,1,0:T(2,128)(2,1)} copy(bf16[1,2,8192]{2,1,0:T(2,128)(2,1)} %shard_map.82) | data formatting | bytes 65536
